TPU v7x, 512 devices: a whole 4x4x16 slice. The times are simulated.
512 devices in a mesh: section: 32 (over z, x_hi), dp: 16 (over y, x_lo, core).
Axes of the slice: x: 4 (x_hi: 2, x_lo: 2; x = x_hi * 2 + x_lo), y: 4, z: 16, core: 2. Of those that a mesh axis runs over, the one named last changes fastest.
Arguments:
- acts: bfloat16 [32, 2048, 5120], P('section', 'dp'), may hold values from -6 to 6
- scores: float32 [32, 32, 64, 64], P('section', 'dp'), may hold values from -10 to 400
- segments: int32 [32, 64], P('dp'), may hold values from 0 to 63, as said below
- cotangent: bfloat16 [2048, 5120], P('dp'), may hold values from -6 to 6
- w_value: bfloat16 [32, 5120, 128], P('section', 'dp'), may hold values from -0.078125 to 0.078125
- w_out: bfloat16 [32, 5120, 128], P('section', 'dp'), may hold values from -0.25 to 0.25
Outputs:
- grad_input: bfloat16 [32, 2048, 5120], P('section', 'dp')
- grad_value: float32 [32, 5120, 128], P('section', 'dp')
- grad_out: float32 [32, 5120, 128], P('section', 'dp')
Inputs may be any that keep to these rules, and one draw needn't show every extreme that they name: `segments`: document ids start at 0 in each sequence, never fall along it and rise by at most one from a token to the next.
All inputs are finite; a program needn't handle non-finite values.
Results may differ from a plain program's by a relative error of at most 0.04.
Values may be sent and summed in bfloat16 or wider, within the bound.
A program may use at most 64 MiB of HBM per device.

v0:
```python
import jax
import jax.numpy as jnp
from jax import lax
from jax.sharding import PartitionSpec as P


def from_behind(array, axis, by):
    peers = lax.axis_size(axis)
    pairs = [(i, i + by) for i in range(peers) if 0 <= i + by < peers]
    return lax.ppermute(array, axis, pairs)


def masked_probs(logits, doc_ids):
    seq_len = logits.shape[-1]
    places = jnp.arange(seq_len)
    allowed = (places[None, :, None] >= places[None, None, :]) & (
        doc_ids[:, :, None] == doc_ids[:, None, :]
    )
    kept = jnp.where(allowed, logits, -jnp.inf)
    row_top = jnp.max(kept, axis=-1, keepdims=True)
    expo = jnp.where(allowed, jnp.exp(kept - row_top), jnp.zeros_like(logits))
    return (expo / jnp.sum(expo, axis=-1, keepdims=True)).astype(jnp.bfloat16)


def shards(acts, scores, segments, cotangent, w_value, w_out):
    n_section = lax.axis_size("section")
    section_id = lax.axis_index("section")
    tokens = acts[0]
    row_count, feat_width = tokens.shape
    micro_count, seq_len = segments.shape
    head_size = w_value.shape[2]
    value_full, out_full = (
        lax.all_gather(w_value[0], "dp", axis=0, tiled=True),
        lax.all_gather(w_out[0], "dp", axis=0, tiled=True),
    )
    probs = masked_probs(scores[0], segments)
    projected_output = jnp.dot(tokens, value_full, preferred_element_type=jnp.float32).astype(
        jnp.bfloat16
    )
    mixed_values = jnp.einsum(
        "xzj,xjs->xzs",
        probs,
        projected_output.reshape(micro_count, seq_len, head_size),
        preferred_element_type=jnp.float32,
    ).astype(jnp.bfloat16)
    mixed_values = mixed_values.reshape(row_count, head_size)
    cot_blocks = cotangent.reshape(micro_count, seq_len, feat_width)
    last_section = n_section - 1

    def advance(turn, carry):
        incoming, grads_in, value_backs, grads_res = carry
        position = turn - (last_section - section_id)
        active_now = (position >= 0) & (position < micro_count)
        slot_index = jnp.clip(position, 0, micro_count - 1)
        own_rows = lax.dynamic_index_in_dim(cot_blocks, slot_index, 0, keepdims=False)
        current = jnp.where(section_id == last_section, own_rows, incoming)
        probs_now = lax.dynamic_index_in_dim(probs, slot_index, 0, keepdims=False)
        head_gradient = jnp.dot(current, out_full, preferred_element_type=jnp.float32).astype(
            jnp.bfloat16
        )
        value_gradient = jnp.einsum(
            "qk,qh->kh", probs_now, head_gradient, preferred_element_type=jnp.float32
        ).astype(jnp.bfloat16)
        spread = lax.dot_general(
            value_gradient, value_full, (((1,), (1,)), ((), ())), preferred_element_type=jnp.float32
        )
        result = (current.astype(jnp.float32) + spread).astype(jnp.bfloat16)

        def store(buffer, fresh):
            previous = lax.dynamic_index_in_dim(buffer, slot_index, 0, keepdims=True)
            return lax.dynamic_update_index_in_dim(
                buffer, jnp.where(active_now, fresh[None], previous), slot_index, 0
            )

        grads_in = store(grads_in, current)
        value_backs = store(value_backs, value_gradient)
        grads_res = store(grads_res, result)
        incoming = from_behind(result, "section", -1)
        return (incoming, grads_in, value_backs, grads_res)

    start_carry = (
        jnp.zeros((seq_len, feat_width), jnp.bfloat16),
        jnp.zeros((micro_count, seq_len, feat_width), jnp.bfloat16),
        jnp.zeros((micro_count, seq_len, head_size), jnp.bfloat16),
        jnp.zeros((micro_count, seq_len, feat_width), jnp.bfloat16),
    )
    final_carry = lax.fori_loop(0, n_section + micro_count - 1, advance, start_carry)
    grads_flat = final_carry[1].reshape(row_count, feat_width)
    backs_flat = final_carry[2].reshape(row_count, head_size)
    grad_input = final_carry[3].reshape(1, row_count, feat_width)
    columns = grads_flat
    grad_out = lax.psum_scatter(
        lax.dot_general(
            columns, mixed_values, (((0,), (0,)), ((), ())), preferred_element_type=jnp.float32
        ).astype(jnp.bfloat16),
        "dp",
        scatter_dimension=0,
        tiled=True,
    ).astype(jnp.float32)
    columns = tokens
    grad_value = lax.psum_scatter(
        lax.dot_general(
            columns, backs_flat, (((0,), (0,)), ((), ())), preferred_element_type=jnp.float32
        ).astype(jnp.bfloat16),
        "dp",
        scatter_dimension=0,
        tiled=True,
    ).astype(jnp.float32)
    return (grad_input, grad_value[None], grad_out[None])


def solution(mesh):
    placed = (
        P("section", "dp", None),
        P("section", "dp", None, None),
        P("dp", None),
        P("dp", None),
        P("section", "dp", None),
        P("section", "dp", None),
    )
    return jax.shard_map(
        shards,
        mesh=mesh,
        in_specs=placed,
        out_specs=(P("section", "dp", None), P("section", "dp", None), P("section", "dp", None)),
        check_vma=False,
    )
```

profile of v0, /device:TPU:32, one launch (start us, length us, event | category | flops | bytes accessed | tf_op | source)
XLA Modules:
  0.0 1126.5 jit_solution(2776788827012103360)
XLA Ops:
  10.7 44.2 %all-gather.7.cloned.1.call-done = bf16[1,5120,128]{2,1,0:T(8,128)(2,1)} async-done(((bf16[1,320,128]{2,1,0:T(8,128)(2,1)}), bf16[1,5120,128]{2,1,0:T(8,128)(2,1)}) %all-gather.7.cloned.1.call-update) | async-done | bytes 1310736 | tf_op jit(solution)/shard_map/all_gather | solution.py:33
  54.9 42.9 %all-gather.5.cloned.1.call-done = bf16[1,5120,128]{2,1,0:T(8,128)(2,1)} async-done(((bf16[1,320,128]{2,1,0:T(8,128)(2,1)}), bf16[1,5120,128]{2,1,0:T(8,128)(2,1)}) %all-gather.5.cloned.1.call-update) | async-done | bytes 1310736 | tf_op jit(solution)/shard_map/all_gather | solution.py:34
  101.1 858.5 %while.21 = (s32[]{:T(128)}, bf16[64,5120]{1,0:T(8,128)(2,1)}, bf16[2,64,5120]{2,1,0:T(8,128)(2,1)}, bf16[2,64,128]{2,1,0:T(8,128)(2,1)S(1)}, bf16[2,64,5120]{2,...) while((s32[]{:T(128)}, bf16[64,5120]{1,0:T(8,128)(2,1)}, ...), condition=%wide.region_3.4_spmd, body=%wide.region_2.3_spmd.sunk | while | flops 170811392 | bytes 14502156 | solution.py:87
  112.8 15.9 %collective-permute-done = bf16[64,5120]{1,0:T(8,128)(2,1)S(1)} collective-permute-done((bf16[64,5120]{1,0:T(8,128)(2,1)}, bf16[64,5120]{1,0:T(8,128)(2,1)S(1)}, u32[]{:S(2)}, u32[]{:S(2)}) %collective-permute-start) | collective-permute-done | bytes 655392 | tf_op jit(solution)/shard_map/while/body/eval_jaxpr/ppermute | solution.py:10
  142.1 14.6 %collective-permute-done = bf16[64,5120]{1,0:T(8,128)(2,1)S(1)} collective-permute-done((bf16[64,5120]{1,0:T(8,128)(2,1)}, bf16[64,5120]{1,0:T(8,128)(2,1)S(1)}, u32[]{:S(2)}, u32[]{:S(2)}) %collective-permute-start) | collective-permute-done | bytes 655392 | tf_op jit(solution)/shard_map/while/body/eval_jaxpr/ppermute | solution.py:10
  170.6 13.7 %collective-permute-done = bf16[64,5120]{1,0:T(8,128)(2,1)S(1)} collective-permute-done((bf16[64,5120]{1,0:T(8,128)(2,1)}, bf16[64,5120]{1,0:T(8,128)(2,1)S(1)}, u32[]{:S(2)}, u32[]{:S(2)}) %collective-permute-start) | collective-permute-done | bytes 655392 | tf_op jit(solution)/shard_map/while/body/eval_jaxpr/ppermute | solution.py:10
  198.3 12.8 %collective-permute-done = bf16[64,5120]{1,0:T(8,128)(2,1)S(1)} collective-permute-done((bf16[64,5120]{1,0:T(8,128)(2,1)}, bf16[64,5120]{1,0:T(8,128)(2,1)S(1)}, u32[]{:S(2)}, u32[]{:S(2)}) %collective-permute-start) | collective-permute-done | bytes 655392 | tf_op jit(solution)/shard_map/while/body/eval_jaxpr/ppermute | solution.py:10
  224.9 11.9 %collective-permute-done = bf16[64,5120]{1,0:T(8,128)(2,1)S(1)} collective-permute-done((bf16[64,5120]{1,0:T(8,128)(2,1)}, bf16[64,5120]{1,0:T(8,128)(2,1)S(1)}, u32[]{:S(2)}, u32[]{:S(2)}) %collective-permute-start) | collective-permute-done | bytes 655392 | tf_op jit(solution)/shard_map/while/body/eval_jaxpr/ppermute | solution.py:10
  250.7 10.9 collective-permute-done
  275.6 10.0 collective-permute-done
  437.8 11.0 collective-permute-done
  460.8 12.2 %collective-permute-done = bf16[64,5120]{1,0:T(8,128)(2,1)S(1)} collective-permute-done((bf16[64,5120]{1,0:T(8,128)(2,1)}, bf16[64,5120]{1,0:T(8,128)(2,1)S(1)}, u32[]{:S(2)}, u32[]{:S(2)}) %collective-permute-start) | collective-permute-done | bytes 655392 | tf_op jit(solution)/shard_map/while/body/eval_jaxpr/ppermute | solution.py:10
  483.9 13.4 %collective-permute-done = bf16[64,5120]{1,0:T(8,128)(2,1)S(1)} collective-permute-done((bf16[64,5120]{1,0:T(8,128)(2,1)}, bf16[64,5120]{1,0:T(8,128)(2,1)S(1)}, u32[]{:S(2)}, u32[]{:S(2)}) %collective-permute-start) | collective-permute-done | bytes 655392 | tf_op jit(solution)/shard_map/while/body/eval_jaxpr/ppermute | solution.py:10
  507.1 14.4 %collective-permute-done = bf16[64,5120]{1,0:T(8,128)(2,1)S(1)} collective-permute-done((bf16[64,5120]{1,0:T(8,128)(2,1)}, bf16[64,5120]{1,0:T(8,128)(2,1)S(1)}, u32[]{:S(2)}, u32[]{:S(2)}) %collective-permute-start) | collective-permute-done | bytes 655392 | tf_op jit(solution)/shard_map/while/body/eval_jaxpr/ppermute | solution.py:10
  531.4 15.6 %collective-permute-done = bf16[64,5120]{1,0:T(8,128)(2,1)S(1)} collective-permute-done((bf16[64,5120]{1,0:T(8,128)(2,1)}, bf16[64,5120]{1,0:T(8,128)(2,1)S(1)}, u32[]{:S(2)}, u32[]{:S(2)}) %collective-permute-start) | collective-permute-done | bytes 655392 | tf_op jit(solution)/shard_map/while/body/eval_jaxpr/ppermute | solution.py:10
  556.9 17.0 %collective-permute-done = bf16[64,5120]{1,0:T(8,128)(2,1)S(1)} collective-permute-done((bf16[64,5120]{1,0:T(8,128)(2,1)}, bf16[64,5120]{1,0:T(8,128)(2,1)S(1)}, u32[]{:S(2)}, u32[]{:S(2)}) %collective-permute-start) | collective-permute-done | bytes 655392 | tf_op jit(solution)/shard_map/while/body/eval_jaxpr/ppermute | solution.py:10
  583.8 18.4 %collective-permute-done = bf16[64,5120]{1,0:T(8,128)(2,1)S(1)} collective-permute-done((bf16[64,5120]{1,0:T(8,128)(2,1)}, bf16[64,5120]{1,0:T(8,128)(2,1)S(1)}, u32[]{:S(2)}, u32[]{:S(2)}) %collective-permute-start) | collective-permute-done | bytes 655392 | tf_op jit(solution)/shard_map/while/body/eval_jaxpr/ppermute | solution.py:10
  612.1 19.6 %collective-permute-done = bf16[64,5120]{1,0:T(8,128)(2,1)S(1)} collective-permute-done((bf16[64,5120]{1,0:T(8,128)(2,1)}, bf16[64,5120]{1,0:T(8,128)(2,1)S(1)}, u32[]{:S(2)}, u32[]{:S(2)}) %collective-permute-start) | collective-permute-done | bytes 655392 | tf_op jit(solution)/shard_map/while/body/eval_jaxpr/ppermute | solution.py:10
  641.5 21.1 %collective-permute-done = bf16[64,5120]{1,0:T(8,128)(2,1)S(1)} collective-permute-done((bf16[64,5120]{1,0:T(8,128)(2,1)}, bf16[64,5120]{1,0:T(8,128)(2,1)S(1)}, u32[]{:S(2)}, u32[]{:S(2)}) %collective-permute-start) | collective-permute-done | bytes 655392 | tf_op jit(solution)/shard_map/while/body/eval_jaxpr/ppermute | solution.py:10
  672.5 22.2 %collective-permute-done = bf16[64,5120]{1,0:T(8,128)(2,1)S(1)} collective-permute-done((bf16[64,5120]{1,0:T(8,128)(2,1)}, bf16[64,5120]{1,0:T(8,128)(2,1)S(1)}, u32[]{:S(2)}, u32[]{:S(2)}) %collective-permute-start) | collective-permute-done | bytes 655392 | tf_op jit(solution)/shard_map/while/body/eval_jaxpr/ppermute | solution.py:10
  704.6 22.2 %collective-permute-done = bf16[64,5120]{1,0:T(8,128)(2,1)S(1)} collective-permute-done((bf16[64,5120]{1,0:T(8,128)(2,1)}, bf16[64,5120]{1,0:T(8,128)(2,1)S(1)}, u32[]{:S(2)}, u32[]{:S(2)}) %collective-permute-start) | collective-permute-done | bytes 655392 | tf_op jit(solution)/shard_map/while/body/eval_jaxpr/ppermute | solution.py:10
  736.7 21.3 %collective-permute-done = bf16[64,5120]{1,0:T(8,128)(2,1)S(1)} collective-permute-done((bf16[64,5120]{1,0:T(8,128)(2,1)}, bf16[64,5120]{1,0:T(8,128)(2,1)S(1)}, u32[]{:S(2)}, u32[]{:S(2)}) %collective-permute-start) | collective-permute-done | bytes 655392 | tf_op jit(solution)/shard_map/while/body/eval_jaxpr/ppermute | solution.py:10
  767.9 19.2 %collective-permute-done = bf16[64,5120]{1,0:T(8,128)(2,1)S(1)} collective-permute-done((bf16[64,5120]{1,0:T(8,128)(2,1)}, bf16[64,5120]{1,0:T(8,128)(2,1)S(1)}, u32[]{:S(2)}, u32[]{:S(2)}) %collective-permute-start) | collective-permute-done | bytes 655392 | tf_op jit(solution)/shard_map/while/body/eval_jaxpr/ppermute | solution.py:10
  797.0 17.6 %collective-permute-done = bf16[64,5120]{1,0:T(8,128)(2,1)S(1)} collective-permute-done((bf16[64,5120]{1,0:T(8,128)(2,1)}, bf16[64,5120]{1,0:T(8,128)(2,1)S(1)}, u32[]{:S(2)}, u32[]{:S(2)}) %collective-permute-start) | collective-permute-done | bytes 655392 | tf_op jit(solution)/shard_map/while/body/eval_jaxpr/ppermute | solution.py:10
  824.5 16.0 %collective-permute-done = bf16[64,5120]{1,0:T(8,128)(2,1)S(1)} collective-permute-done((bf16[64,5120]{1,0:T(8,128)(2,1)}, bf16[64,5120]{1,0:T(8,128)(2,1)S(1)}, u32[]{:S(2)}, u32[]{:S(2)}) %collective-permute-start) | collective-permute-done | bytes 655392 | tf_op jit(solution)/shard_map/while/body/eval_jaxpr/ppermute | solution.py:10
  850.9 14.6 %collective-permute-done = bf16[64,5120]{1,0:T(8,128)(2,1)S(1)} collective-permute-done((bf16[64,5120]{1,0:T(8,128)(2,1)}, bf16[64,5120]{1,0:T(8,128)(2,1)S(1)}, u32[]{:S(2)}, u32[]{:S(2)}) %collective-permute-start) | collective-permute-done | bytes 655392 | tf_op jit(solution)/shard_map/while/body/eval_jaxpr/ppermute | solution.py:10
  876.5 13.1 %collective-permute-done = bf16[64,5120]{1,0:T(8,128)(2,1)S(1)} collective-permute-done((bf16[64,5120]{1,0:T(8,128)(2,1)}, bf16[64,5120]{1,0:T(8,128)(2,1)S(1)}, u32[]{:S(2)}, u32[]{:S(2)}) %collective-permute-start) | collective-permute-done | bytes 655392 | tf_op jit(solution)/shard_map/while/body/eval_jaxpr/ppermute | solution.py:10
  901.1 11.6 %collective-permute-done = bf16[64,5120]{1,0:T(8,128)(2,1)S(1)} collective-permute-done((bf16[64,5120]{1,0:T(8,128)(2,1)}, bf16[64,5120]{1,0:T(8,128)(2,1)S(1)}, u32[]{:S(2)}, u32[]{:S(2)}) %collective-permute-start) | collective-permute-done | bytes 655392 | tf_op jit(solution)/shard_map/while/body/eval_jaxpr/ppermute | solution.py:10
  924.8 10.7 collective-permute-done
  947.8 10.9 collective-permute-done
  967.2 80.2 %reduce-scatter.7.cloned.1.call-done = bf16[320,128]{1,0:T(8,128)(2,1)} async-done(((bf16[5120,128]{1,0:T(8,128)(2,1)}), bf16[320,128]{1,0:T(8,128)(2,1)}) %reduce-scatter.7.cloned.1.call-update) | async-done | bytes 81936
  1049.2 69.2 %reduce-scatter.5.cloned.1.call-done = bf16[320,128]{1,0:T(8,128)(2,1)} async-done(((bf16[5120,128]{1,0:T(8,128)(2,1)}), bf16[320,128]{1,0:T(8,128)(2,1)}) %reduce-scatter.5.cloned.1.call-update) | async-done | bytes 81936 | tf_op jit(solution)/shard_map/reduce_scatter | solution.py:92
  (231 shorter events, 463.4 us)
Async XLA Ops:
  7.2 47.7 %all-gather.7.cloned.1.call-start = ((), (), s32[]{:S(2)}) async-start(), calls=%async_computation.4 | async-start | bytes 1392640 | tf_op jit(solution)/shard_map/all_gather | solution.py:33
  7.9 89.9 %all-gather.5.cloned.1.call-start = ((), (), s32[]{:S(2)}) async-start(), calls=%async_computation.3 | async-start | bytes 1392640 | tf_op jit(solution)/shard_map/all_gather | solution.py:34
  8.7 1038.7 %reduce-scatter.7.cloned.1.call-start = ((), (), s32[]{:S(2)}) async-start(), calls=%async_computation.5 | async-start | bytes 1392640
  108.3 20.5 %collective-permute-start = (bf16[64,5120]{1,0:T(8,128)(2,1)}, bf16[64,5120]{1,0:T(8,128)(2,1)S(1)}, u32[]{:S(2)}, u32[]{:S(2)}) collective-permute-start(bf16[64,5120]{1,0:T(8,128)(2,1)} %get-tuple-element.357), channel_id=1, source_target_pairs={{16,0},{32,16},{48,32},{64,48},{80,64},{96,80},{112,96},{128,112},... | collective-permute-start | bytes 1966088 | tf_op jit(solution)/shard_map/while/body/eval_jaxpr/ppermute | solution.py:10
  136.7 20.1 %collective-permute-start = (bf16[64,5120]{1,0:T(8,128)(2,1)}, bf16[64,5120]{1,0:T(8,128)(2,1)S(1)}, u32[]{:S(2)}, u32[]{:S(2)}) collective-permute-start(bf16[64,5120]{1,0:T(8,128)(2,1)} %get-tuple-element.357), channel_id=1, source_target_pairs={{16,0},{32,16},{48,32},{64,48},{80,64},{96,80},{112,96},{128,112},... | collective-permute-start | bytes 1966088 | tf_op jit(solution)/shard_map/while/body/eval_jaxpr/ppermute | solution.py:10
  164.7 19.6 %collective-permute-start = (bf16[64,5120]{1,0:T(8,128)(2,1)}, bf16[64,5120]{1,0:T(8,128)(2,1)S(1)}, u32[]{:S(2)}, u32[]{:S(2)}) collective-permute-start(bf16[64,5120]{1,0:T(8,128)(2,1)} %get-tuple-element.357), channel_id=1, source_target_pairs={{16,0},{32,16},{48,32},{64,48},{80,64},{96,80},{112,96},{128,112},... | collective-permute-start | bytes 1966088 | tf_op jit(solution)/shard_map/while/body/eval_jaxpr/ppermute | solution.py:10
  192.3 18.7 %collective-permute-start = (bf16[64,5120]{1,0:T(8,128)(2,1)}, bf16[64,5120]{1,0:T(8,128)(2,1)S(1)}, u32[]{:S(2)}, u32[]{:S(2)}) collective-permute-start(bf16[64,5120]{1,0:T(8,128)(2,1)} %get-tuple-element.357), channel_id=1, source_target_pairs={{16,0},{32,16},{48,32},{64,48},{80,64},{96,80},{112,96},{128,112},... | collective-permute-start | bytes 1966088 | tf_op jit(solution)/shard_map/while/body/eval_jaxpr/ppermute | solution.py:10
  219.0 17.8 %collective-permute-start = (bf16[64,5120]{1,0:T(8,128)(2,1)}, bf16[64,5120]{1,0:T(8,128)(2,1)S(1)}, u32[]{:S(2)}, u32[]{:S(2)}) collective-permute-start(bf16[64,5120]{1,0:T(8,128)(2,1)} %get-tuple-element.357), channel_id=1, source_target_pairs={{16,0},{32,16},{48,32},{64,48},{80,64},{96,80},{112,96},{128,112},... | collective-permute-start | bytes 1966088 | tf_op jit(solution)/shard_map/while/body/eval_jaxpr/ppermute | solution.py:10
  244.8 16.9 %collective-permute-start = (bf16[64,5120]{1,0:T(8,128)(2,1)}, bf16[64,5120]{1,0:T(8,128)(2,1)S(1)}, u32[]{:S(2)}, u32[]{:S(2)}) collective-permute-start(bf16[64,5120]{1,0:T(8,128)(2,1)} %get-tuple-element.357), channel_id=1, source_target_pairs={{16,0},{32,16},{48,32},{64,48},{80,64},{96,80},{112,96},{128,112},... | collective-permute-start | bytes 1966088 | tf_op jit(solution)/shard_map/while/body/eval_jaxpr/ppermute | solution.py:10
  269.6 16.0 %collective-permute-start = (bf16[64,5120]{1,0:T(8,128)(2,1)}, bf16[64,5120]{1,0:T(8,128)(2,1)S(1)}, u32[]{:S(2)}, u32[]{:S(2)}) collective-permute-start(bf16[64,5120]{1,0:T(8,128)(2,1)} %get-tuple-element.357), channel_id=1, source_target_pairs={{16,0},{32,16},{48,32},{64,48},{80,64},{96,80},{112,96},{128,112},... | collective-permute-start | bytes 1966088 | tf_op jit(solution)/shard_map/while/body/eval_jaxpr/ppermute | solution.py:10
  339.4 15.1 %collective-permute-start = (bf16[64,5120]{1,0:T(8,128)(2,1)}, bf16[64,5120]{1,0:T(8,128)(2,1)S(1)}, u32[]{:S(2)}, u32[]{:S(2)}) collective-permute-start(bf16[64,5120]{1,0:T(8,128)(2,1)} %get-tuple-element.357), channel_id=1, source_target_pairs={{16,0},{32,16},{48,32},{64,48},{80,64},{96,80},{112,96},{128,112},... | collective-permute-start | bytes 1966088 | tf_op jit(solution)/shard_map/while/body/eval_jaxpr/ppermute | solution.py:10
  408.5 16.0 %collective-permute-start = (bf16[64,5120]{1,0:T(8,128)(2,1)}, bf16[64,5120]{1,0:T(8,128)(2,1)S(1)}, u32[]{:S(2)}, u32[]{:S(2)}) collective-permute-start(bf16[64,5120]{1,0:T(8,128)(2,1)} %get-tuple-element.357), channel_id=1, source_target_pairs={{16,0},{32,16},{48,32},{64,48},{80,64},{96,80},{112,96},{128,112},... | collective-permute-start | bytes 1966088 | tf_op jit(solution)/shard_map/while/body/eval_jaxpr/ppermute | solution.py:10
  432.4 16.3 %collective-permute-start = (bf16[64,5120]{1,0:T(8,128)(2,1)}, bf16[64,5120]{1,0:T(8,128)(2,1)S(1)}, u32[]{:S(2)}, u32[]{:S(2)}) collective-permute-start(bf16[64,5120]{1,0:T(8,128)(2,1)} %get-tuple-element.357), channel_id=1, source_target_pairs={{16,0},{32,16},{48,32},{64,48},{80,64},{96,80},{112,96},{128,112},... | collective-permute-start | bytes 1966088 | tf_op jit(solution)/shard_map/while/body/eval_jaxpr/ppermute | solution.py:10
  456.7 16.3 %collective-permute-start = (bf16[64,5120]{1,0:T(8,128)(2,1)}, bf16[64,5120]{1,0:T(8,128)(2,1)S(1)}, u32[]{:S(2)}, u32[]{:S(2)}) collective-permute-start(bf16[64,5120]{1,0:T(8,128)(2,1)} %get-tuple-element.357), channel_id=1, source_target_pairs={{16,0},{32,16},{48,32},{64,48},{80,64},{96,80},{112,96},{128,112},... | collective-permute-start | bytes 1966088 | tf_op jit(solution)/shard_map/while/body/eval_jaxpr/ppermute | solution.py:10
  481.0 16.3 %collective-permute-start = (bf16[64,5120]{1,0:T(8,128)(2,1)}, bf16[64,5120]{1,0:T(8,128)(2,1)S(1)}, u32[]{:S(2)}, u32[]{:S(2)}) collective-permute-start(bf16[64,5120]{1,0:T(8,128)(2,1)} %get-tuple-element.357), channel_id=1, source_target_pairs={{16,0},{32,16},{48,32},{64,48},{80,64},{96,80},{112,96},{128,112},... | collective-permute-start | bytes 1966088 | tf_op jit(solution)/shard_map/while/body/eval_jaxpr/ppermute | solution.py:10
  505.2 16.3 %collective-permute-start = (bf16[64,5120]{1,0:T(8,128)(2,1)}, bf16[64,5120]{1,0:T(8,128)(2,1)S(1)}, u32[]{:S(2)}, u32[]{:S(2)}) collective-permute-start(bf16[64,5120]{1,0:T(8,128)(2,1)} %get-tuple-element.357), channel_id=1, source_target_pairs={{16,0},{32,16},{48,32},{64,48},{80,64},{96,80},{112,96},{128,112},... | collective-permute-start | bytes 1966088 | tf_op jit(solution)/shard_map/while/body/eval_jaxpr/ppermute | solution.py:10
  529.5 17.5 %collective-permute-start = (bf16[64,5120]{1,0:T(8,128)(2,1)}, bf16[64,5120]{1,0:T(8,128)(2,1)S(1)}, u32[]{:S(2)}, u32[]{:S(2)}) collective-permute-start(bf16[64,5120]{1,0:T(8,128)(2,1)} %get-tuple-element.357), channel_id=1, source_target_pairs={{16,0},{32,16},{48,32},{64,48},{80,64},{96,80},{112,96},{128,112},... | collective-permute-start | bytes 1966088 | tf_op jit(solution)/shard_map/while/body/eval_jaxpr/ppermute | solution.py:10
  554.9 18.9 %collective-permute-start = (bf16[64,5120]{1,0:T(8,128)(2,1)}, bf16[64,5120]{1,0:T(8,128)(2,1)S(1)}, u32[]{:S(2)}, u32[]{:S(2)}) collective-permute-start(bf16[64,5120]{1,0:T(8,128)(2,1)} %get-tuple-element.357), channel_id=1, source_target_pairs={{16,0},{32,16},{48,32},{64,48},{80,64},{96,80},{112,96},{128,112},... | collective-permute-start | bytes 1966088 | tf_op jit(solution)/shard_map/while/body/eval_jaxpr/ppermute | solution.py:10
  581.9 20.4 %collective-permute-start = (bf16[64,5120]{1,0:T(8,128)(2,1)}, bf16[64,5120]{1,0:T(8,128)(2,1)S(1)}, u32[]{:S(2)}, u32[]{:S(2)}) collective-permute-start(bf16[64,5120]{1,0:T(8,128)(2,1)} %get-tuple-element.357), channel_id=1, source_target_pairs={{16,0},{32,16},{48,32},{64,48},{80,64},{96,80},{112,96},{128,112},... | collective-permute-start | bytes 1966088 | tf_op jit(solution)/shard_map/while/body/eval_jaxpr/ppermute | solution.py:10
  610.2 21.5 %collective-permute-start = (bf16[64,5120]{1,0:T(8,128)(2,1)}, bf16[64,5120]{1,0:T(8,128)(2,1)S(1)}, u32[]{:S(2)}, u32[]{:S(2)}) collective-permute-start(bf16[64,5120]{1,0:T(8,128)(2,1)} %get-tuple-element.357), channel_id=1, source_target_pairs={{16,0},{32,16},{48,32},{64,48},{80,64},{96,80},{112,96},{128,112},... | collective-permute-start | bytes 1966088 | tf_op jit(solution)/shard_map/while/body/eval_jaxpr/ppermute | solution.py:10
  639.6 23.0 %collective-permute-start = (bf16[64,5120]{1,0:T(8,128)(2,1)}, bf16[64,5120]{1,0:T(8,128)(2,1)S(1)}, u32[]{:S(2)}, u32[]{:S(2)}) collective-permute-start(bf16[64,5120]{1,0:T(8,128)(2,1)} %get-tuple-element.357), channel_id=1, source_target_pairs={{16,0},{32,16},{48,32},{64,48},{80,64},{96,80},{112,96},{128,112},... | collective-permute-start | bytes 1966088 | tf_op jit(solution)/shard_map/while/body/eval_jaxpr/ppermute | solution.py:10
  670.6 24.1 %collective-permute-start = (bf16[64,5120]{1,0:T(8,128)(2,1)}, bf16[64,5120]{1,0:T(8,128)(2,1)S(1)}, u32[]{:S(2)}, u32[]{:S(2)}) collective-permute-start(bf16[64,5120]{1,0:T(8,128)(2,1)} %get-tuple-element.357), channel_id=1, source_target_pairs={{16,0},{32,16},{48,32},{64,48},{80,64},{96,80},{112,96},{128,112},... | collective-permute-start | bytes 1966088 | tf_op jit(solution)/shard_map/while/body/eval_jaxpr/ppermute | solution.py:10
  702.7 24.1 %collective-permute-start = (bf16[64,5120]{1,0:T(8,128)(2,1)}, bf16[64,5120]{1,0:T(8,128)(2,1)S(1)}, u32[]{:S(2)}, u32[]{:S(2)}) collective-permute-start(bf16[64,5120]{1,0:T(8,128)(2,1)} %get-tuple-element.357), channel_id=1, source_target_pairs={{16,0},{32,16},{48,32},{64,48},{80,64},{96,80},{112,96},{128,112},... | collective-permute-start | bytes 1966088 | tf_op jit(solution)/shard_map/while/body/eval_jaxpr/ppermute | solution.py:10
  734.8 23.3 %collective-permute-start = (bf16[64,5120]{1,0:T(8,128)(2,1)}, bf16[64,5120]{1,0:T(8,128)(2,1)S(1)}, u32[]{:S(2)}, u32[]{:S(2)}) collective-permute-start(bf16[64,5120]{1,0:T(8,128)(2,1)} %get-tuple-element.357), channel_id=1, source_target_pairs={{16,0},{32,16},{48,32},{64,48},{80,64},{96,80},{112,96},{128,112},... | collective-permute-start | bytes 1966088 | tf_op jit(solution)/shard_map/while/body/eval_jaxpr/ppermute | solution.py:10
  766.0 21.1 %collective-permute-start = (bf16[64,5120]{1,0:T(8,128)(2,1)}, bf16[64,5120]{1,0:T(8,128)(2,1)S(1)}, u32[]{:S(2)}, u32[]{:S(2)}) collective-permute-start(bf16[64,5120]{1,0:T(8,128)(2,1)} %get-tuple-element.357), channel_id=1, source_target_pairs={{16,0},{32,16},{48,32},{64,48},{80,64},{96,80},{112,96},{128,112},... | collective-permute-start | bytes 1966088 | tf_op jit(solution)/shard_map/while/body/eval_jaxpr/ppermute | solution.py:10
  795.1 19.5 %collective-permute-start = (bf16[64,5120]{1,0:T(8,128)(2,1)}, bf16[64,5120]{1,0:T(8,128)(2,1)S(1)}, u32[]{:S(2)}, u32[]{:S(2)}) collective-permute-start(bf16[64,5120]{1,0:T(8,128)(2,1)} %get-tuple-element.357), channel_id=1, source_target_pairs={{16,0},{32,16},{48,32},{64,48},{80,64},{96,80},{112,96},{128,112},... | collective-permute-start | bytes 1966088 | tf_op jit(solution)/shard_map/while/body/eval_jaxpr/ppermute | solution.py:10
  822.6 17.9 %collective-permute-start = (bf16[64,5120]{1,0:T(8,128)(2,1)}, bf16[64,5120]{1,0:T(8,128)(2,1)S(1)}, u32[]{:S(2)}, u32[]{:S(2)}) collective-permute-start(bf16[64,5120]{1,0:T(8,128)(2,1)} %get-tuple-element.357), channel_id=1, source_target_pairs={{16,0},{32,16},{48,32},{64,48},{80,64},{96,80},{112,96},{128,112},... | collective-permute-start | bytes 1966088 | tf_op jit(solution)/shard_map/while/body/eval_jaxpr/ppermute | solution.py:10
  848.5 17.0 %collective-permute-start = (bf16[64,5120]{1,0:T(8,128)(2,1)}, bf16[64,5120]{1,0:T(8,128)(2,1)S(1)}, u32[]{:S(2)}, u32[]{:S(2)}) collective-permute-start(bf16[64,5120]{1,0:T(8,128)(2,1)} %get-tuple-element.357), channel_id=1, source_target_pairs={{16,0},{32,16},{48,32},{64,48},{80,64},{96,80},{112,96},{128,112},... | collective-permute-start | bytes 1966088 | tf_op jit(solution)/shard_map/while/body/eval_jaxpr/ppermute | solution.py:10
  873.5 16.1 %collective-permute-start = (bf16[64,5120]{1,0:T(8,128)(2,1)}, bf16[64,5120]{1,0:T(8,128)(2,1)S(1)}, u32[]{:S(2)}, u32[]{:S(2)}) collective-permute-start(bf16[64,5120]{1,0:T(8,128)(2,1)} %get-tuple-element.357), channel_id=1, source_target_pairs={{16,0},{32,16},{48,32},{64,48},{80,64},{96,80},{112,96},{128,112},... | collective-permute-start | bytes 1966088 | tf_op jit(solution)/shard_map/while/body/eval_jaxpr/ppermute | solution.py:10
  897.5 15.2 %collective-permute-start = (bf16[64,5120]{1,0:T(8,128)(2,1)}, bf16[64,5120]{1,0:T(8,128)(2,1)S(1)}, u32[]{:S(2)}, u32[]{:S(2)}) collective-permute-start(bf16[64,5120]{1,0:T(8,128)(2,1)} %get-tuple-element.357), channel_id=1, source_target_pairs={{16,0},{32,16},{48,32},{64,48},{80,64},{96,80},{112,96},{128,112},... | collective-permute-start | bytes 1966088 | tf_op jit(solution)/shard_map/while/body/eval_jaxpr/ppermute | solution.py:10
  943.5 15.3 %collective-permute-start = (bf16[64,5120]{1,0:T(8,128)(2,1)}, bf16[64,5120]{1,0:T(8,128)(2,1)S(1)}, u32[]{:S(2)}, u32[]{:S(2)}) collective-permute-start(bf16[64,5120]{1,0:T(8,128)(2,1)} %get-tuple-element.357), channel_id=1, source_target_pairs={{16,0},{32,16},{48,32},{64,48},{80,64},{96,80},{112,96},{128,112},... | collective-permute-start | bytes 1966088 | tf_op jit(solution)/shard_map/while/body/eval_jaxpr/ppermute | solution.py:10
  963.6 154.8 %reduce-scatter.5.cloned.1.call-start = ((), (), s32[]{:S(2)}) async-start(), calls=%async_computation.2 | async-start | bytes 1392640 | tf_op jit(solution)/shard_map/reduce_scatter | solution.py:92
  (40 other events, 1056.9 us)
Sparse Core Ops, SparseCore 0:
  10.2 44.7 all-gather.6
  57.0 40.7 all-gather.4
  963.7 83.6 reduce-scatter.6
  1050.0 68.2 reduce-scatter.4
where the time goes:
time: 1130 us
  waiting for transfers between devices  704 us (62%)
  matrix products  154 us (14%)
  starting transfers between devices  129 us (11%)
  other arithmetic  89.4 us (8%)
  local copies, waits for them, and re-layouts  35 us (3%)
  between operations  13.8 us (1%)
    ppermute x33, waiting for transfers between devices, from_behind(): return lax.ppermute(array, axis, pairs)  466 us
    ppermute x33, starting transfers between devices, from_behind(): return lax.ppermute(array, axis, pairs)  129 us
    dot_general x33, matrix products, advance(): lax.dot_general(value_gradient, value_full, (((1,), (1,)), ((), ())), pre...  89.9 us
    dynamic_update_slice x33, other arithmetic, store(): lax.dynamic_update_index_in_dim(buffer, jnp.where(active_now, fresh[None]...  85.9 us
    unnamed x5, waiting for transfers between devices  81.6 us
    reduce_scatter x1, waiting for transfers between devices, shards(): lax.psum_scatter(lax.dot_general(columns, mixed_values, (((0,), (0,)), ((...  69.2 us
    dot_general x33, matrix products, advance(): jnp.einsum('qk,qh->kh', probs_now, head_gradient, preferred_element_type=...  59.2 us
    all_gather x1, waiting for transfers between devices, shards(): lax.all_gather(w_value[0], 'dp', axis=0, tiled=True)  44.2 us
  transfers between devices with their start and end apart: 37, of which 37 were waited for; matrix products, arithmetic and copies ran while one was open for 1% of the time, Pallas kernels for 0%

commit v1 on v0

v1 whole, which is shorter than its diff:
```python
import functools

import jax
import jax.numpy as jnp
from jax import lax
from jax.experimental import pallas as pl
from jax.experimental.pallas import tpu as pltpu
from jax.sharding import PartitionSpec as P

MESH = pl.DeviceIdType.MESH
F32 = jnp.float32
BF16 = jnp.bfloat16


def masked_probs(logits, doc_ids):
    seq_len = logits.shape[-1]
    places = jnp.arange(seq_len)
    allowed = (places[None, :, None] >= places[None, None, :]) & (
        doc_ids[:, :, None] == doc_ids[:, None, :]
    )
    kept = jnp.where(allowed, logits, -jnp.inf)
    row_top = jnp.max(kept, axis=-1, keepdims=True)
    expo = jnp.where(allowed, jnp.exp(kept - row_top), jnp.zeros_like(logits))
    return (expo / jnp.sum(expo, axis=-1, keepdims=True)).astype(BF16)


def chain_kernel(
    n_z,
    chunk_count,
    heads_ref,
    probs_ref,
    cross_ref,
    spread_ref,
    cot_ref,
    grad_ref,
    above_ref,
    middle_ref,
    backs_ref,
    line,
    below,
    other,
    delta_low,
    delta_mid,
    line_send,
    line_recv,
    pair_send,
    pair_recv,
    wave_send,
    wave_recv,
    out_send,
    out_recv,
    cot_sem,
):
    section = lax.axis_index("section")
    z, side = section // 2, section % 2
    rows, width = heads_ref.shape
    head = width // 2
    chunk = spread_ref.shape[2]
    half = chunk * chunk_count
    lower = {"section": lax.rem(z + n_z - 1, n_z) * 2 + side}
    upper = {"section": lax.rem(z + 1, n_z) * 2 + side}
    partner = {"section": z * 2 + 1 - side}

    barrier = pltpu.get_barrier_semaphore()
    for device in (lower, upper, partner):
        pl.semaphore_signal(barrier, inc=1, device_id=device, device_id_type=MESH)
    pl.semaphore_wait(barrier, 3)

    def cot_copy(k):
        columns = pl.ds(pl.multiple_of(side * half + k * chunk, 128), chunk)
        return pltpu.make_async_copy(cot_ref.at[:, columns], above_ref.at[k], cot_sem.at[k])

    @pl.when(z == n_z - 1)
    def _():
        for k in range(chunk_count):
            cot_copy(k).start()

    def line_copy(slot):
        return pltpu.make_async_remote_copy(
            src_ref=line.at[slot],
            dst_ref=line.at[slot],
            send_sem=line_send.at[slot],
            recv_sem=line_recv.at[slot],
            device_id=lower,
            device_id_type=MESH,
        )

    def wave_copy(k):
        return pltpu.make_async_remote_copy(
            src_ref=below.at[k],
            dst_ref=above_ref.at[k],
            send_sem=wave_send.at[k],
            recv_sem=wave_recv.at[k],
            device_id=lower,
            device_id_type=MESH,
        )

    def out_copy(k):
        columns = pl.ds(pl.multiple_of(side * half + k * chunk, 128), chunk)
        return pltpu.make_async_remote_copy(
            src_ref=other.at[k],
            dst_ref=grad_ref.at[:, columns],
            send_sem=out_send.at[k],
            recv_sem=out_recv.at[k],
            device_id=partner,
            device_id_type=MESH,
        )

    def take(i, total):
        slot = n_z - 1 - i
        line_copy(slot).wait_recv()

        @pl.when(z > 0)
        def _():
            line_copy(slot).start()

        return total + jnp.dot(line[slot], cross_ref[slot], preferred_element_type=F32)

    total = lax.fori_loop(0, n_z - 1 - z, take, heads_ref[...])
    back_top = jnp.dot(
        probs_ref[1], total[:, head:].astype(BF16), preferred_element_type=F32
    ).astype(BF16)
    low = total[:, :head] + jnp.dot(
        back_top, cross_ref[z, head:, :head], preferred_element_type=F32
    )
    back_low = jnp.dot(probs_ref[0], low.astype(BF16), preferred_element_type=F32).astype(BF16)
    line[z, :, :head] = back_low
    line[z, :, head:] = back_top

    @pl.when(z > 0)
    def _():
        line_copy(z).start()

    own_rows = pl.ds(pl.multiple_of(side * rows, rows), rows)
    backs_ref[own_rows, :head] = back_low
    backs_ref[own_rows, head:] = back_top
    swap = pltpu.make_async_remote_copy(
        src_ref=backs_ref.at[own_rows],
        dst_ref=backs_ref.at[own_rows],
        send_sem=pair_send,
        recv_sem=pair_recv,
        device_id=partner,
        device_id_type=MESH,
    )
    swap.start()
    swap.wait_send()
    other_rows = pl.ds(pl.multiple_of((1 - side) * rows, rows), rows)
    pltpu.make_async_remote_copy(
        src_ref=backs_ref.at[own_rows],
        dst_ref=backs_ref.at[other_rows],
        send_sem=pair_send,
        recv_sem=pair_recv,
        device_id=partner,
        device_id_type=MESH,
    ).wait_recv()

    for k in range(chunk_count):
        delta_low[k] = jnp.dot(backs_ref[...], spread_ref[k], preferred_element_type=F32)
        delta_mid[k] = jnp.dot(
            backs_ref[:, head:], spread_ref[k, head:, :], preferred_element_type=F32
        )

    for k in range(chunk_count):

        @pl.when(z == n_z - 1)
        def _():
            cot_copy(k).wait()

        @pl.when(z < n_z - 1)
        def _():
            wave_copy(k).wait_recv()

        above = above_ref[k].astype(F32)
        low = (above + delta_low[k]).astype(BF16)
        middle = (above + delta_mid[k]).astype(BF16)
        below[k] = low

        @pl.when(z > 0)
        def _():
            wave_copy(k).start()

        middle_ref[k] = middle
        columns = pl.ds(pl.multiple_of(side * half + k * chunk, 128), chunk)
        grad_ref[:, columns] = jnp.where(side == 1, middle, low)
        other[k] = jnp.where(side == 1, low, middle)
        out_copy(k).start()

    for k in range(chunk_count):
        out_copy(k).wait_send()
        columns = pl.ds(pl.multiple_of((1 - side) * half + k * chunk, 128), chunk)
        pltpu.make_async_remote_copy(
            src_ref=other.at[k],
            dst_ref=grad_ref.at[:, columns],
            send_sem=out_send.at[k],
            recv_sem=out_recv.at[k],
            device_id=partner,
            device_id_type=MESH,
        ).wait_recv()

    @pl.when(z > 0)
    def _():
        for k in range(chunk_count):
            wave_copy(k).wait_send()

        def drain(i, carry):
            line_copy(n_z - 1 - i).wait_send()
            return carry

        lax.fori_loop(0, n_z - z, drain, 0)


def scatter_kernel(n_dp, out_ref, value_ref, sum_out_ref, sum_value_ref, got_out, got_value, out_send, out_recv, value_send, value_recv):
    section = lax.axis_index("section")
    me = lax.axis_index("dp")
    z, side = section // 2, section % 2
    rows = sum_out_ref.shape[0]
    half_dp = n_dp // 2
    source = me // half_dp

    barrier = pltpu.get_barrier_semaphore()
    for other in (0, 1):
        for step in range(n_dp):
            if other or step:
                pl.semaphore_signal(
                    barrier,
                    inc=1,
                    device_id={"section": z * 2 + (side + other) % 2, "dp": lax.rem(me + step, n_dp)},
                    device_id_type=MESH,
                )
    pl.semaphore_wait(barrier, 2 * n_dp - 1)

    def value_copy(step, to):
        return pltpu.make_async_remote_copy(
            src_ref=value_ref.at[pl.ds(pl.multiple_of(to * rows, 16), rows)],
            dst_ref=got_value.at[step],
            send_sem=value_send.at[step],
            recv_sem=value_recv.at[step],
            device_id={"section": section, "dp": to},
            device_id_type=MESH,
        )

    def out_copy(layer, i):
        return pltpu.make_async_remote_copy(
            src_ref=out_ref.at[layer, pl.ds(i * rows, rows)],
            dst_ref=got_out.at[me],
            send_sem=out_send.at[layer, i],
            recv_sem=out_recv.at[me],
            device_id={"section": z * 2 + layer, "dp": side * half_dp + i},
            device_id_type=MESH,
        )

    def self_copy(i):
        return pltpu.make_async_copy(out_ref.at[side, pl.ds(i * rows, rows)], got_out.at[me], out_recv.at[me])

    for layer in (0, 1):
        for i in range(half_dp):
            own = (layer == side) & (side * half_dp + i == me)

            @pl.when(jnp.logical_not(own))
            def _():
                out_copy(layer, i).start()

            @pl.when(own)
            def _():
                self_copy(i).start()

    for step in range(1, n_dp):
        value_copy(step, lax.rem(me + step, n_dp)).start()

    total = value_ref[pl.ds(pl.multiple_of(me * rows, 16), rows)].astype(F32)
    for step in range(1, n_dp):
        value_copy(step, lax.rem(me + step, n_dp)).wait_recv()
        total = total + got_value[step].astype(F32)
    sum_value_ref[...] = total

    for peer in range(n_dp):
        own = (source == side) & (peer == me)

        @pl.when(jnp.logical_not(own))
        def _():
            pltpu.make_async_remote_copy(
                src_ref=out_ref.at[0, pl.ds(0, rows)],
                dst_ref=got_out.at[peer],
                send_sem=out_send.at[0, 0],
                recv_sem=out_recv.at[peer],
                device_id={"section": z * 2 + source, "dp": peer},
                device_id_type=MESH,
            ).wait_recv()

        @pl.when(own)
        def _():
            self_copy(0).wait()

    total = got_out[0].astype(F32)
    for peer in range(1, n_dp):
        total = total + got_out[peer].astype(F32)
    sum_out_ref[...] = total

    for step in range(1, n_dp):
        value_copy(step, lax.rem(me + step, n_dp)).wait_send()
    for layer in (0, 1):
        for i in range(half_dp):
            own = (layer == side) & (side * half_dp + i == me)

            @pl.when(jnp.logical_not(own))
            def _():
                out_copy(layer, i).wait_send()


def shards(acts, scores, segments, cotangent, w_value, w_out):
    n_section = lax.axis_size("section")
    n_dp = lax.axis_size("dp")
    n_z = n_section // 2
    section = lax.axis_index("section")
    side = section % 2
    tokens = acts[0]
    row_count, feat_width = tokens.shape
    micro_count, seq_len = segments.shape
    shard_rows, head = w_value.shape[1:]
    half = feat_width // 2
    chunk = 256 if half % 256 == 0 else 128
    chunk_count = half // chunk

    def swapped(array):
        return lax.ppermute(array, "section", [(i, i ^ 1) for i in range(n_section)])

    def ordered(mine, others, axis):
        return jnp.where(
            side == 0,
            jnp.concatenate([mine, others], axis),
            jnp.concatenate([others, mine], axis),
        )

    value_full = lax.all_gather(w_value[0], "dp", axis=0, tiled=True)
    out_full = lax.all_gather(w_out[0], "dp", axis=0, tiled=True)
    value_layers = lax.all_gather(w_value[0], "section", axis=0)
    cross = lax.psum(
        jnp.einsum("tdk,dj->tkj", value_layers, w_out[0], preferred_element_type=F32).astype(BF16),
        "dp",
    ).reshape(n_z, 2 * head, head)
    cross = ordered(cross, swapped(cross), 2)

    probs = masked_probs(scores[0], segments)
    probs_turned = jnp.swapaxes(probs, 1, 2)
    projected = jnp.dot(tokens, value_full, preferred_element_type=F32).astype(BF16)
    mixed = jnp.einsum(
        "xzj,xjs->xzs",
        probs,
        projected.reshape(micro_count, seq_len, head),
        preferred_element_type=F32,
    ).astype(BF16).reshape(row_count, head)
    heads = jnp.dot(cotangent, out_full, preferred_element_type=F32).reshape(micro_count, seq_len, head)

    def picked(array, index):
        return lax.dynamic_index_in_dim(array, index, 0, keepdims=False)

    heads = ordered(picked(heads, side), swapped(picked(heads, 1 - side)), 1)
    turned = ordered(picked(probs_turned, side)[None], swapped(picked(probs_turned, 1 - side))[None], 0)
    halves = value_full.reshape(2, half, head)
    spread = ordered(picked(halves, side), swapped(picked(halves, 1 - side)), 1)
    spread = jnp.swapaxes(spread.reshape(chunk_count, chunk, 2 * head), 1, 2)
    mixed_pair = ordered(mixed[None], swapped(mixed)[None], 0)

    vmem = pl.BlockSpec(memory_space=pltpu.VMEM)
    grad_input, above, middle, backs = pl.pallas_call(
        functools.partial(chain_kernel, n_z, chunk_count),
        out_shape=(
            jax.ShapeDtypeStruct((row_count, feat_width), BF16),
            jax.ShapeDtypeStruct((chunk_count, row_count, chunk), BF16),
            jax.ShapeDtypeStruct((chunk_count, row_count, chunk), BF16),
            jax.ShapeDtypeStruct((row_count, 2 * head), BF16),
        ),
        in_specs=[vmem] * 4 + [pl.BlockSpec(memory_space=pl.ANY)],
        out_specs=(vmem,) * 4,
        scratch_shapes=[
            pltpu.VMEM((n_z, seq_len, 2 * head), BF16),
            pltpu.VMEM((chunk_count, row_count, chunk), BF16),
            pltpu.VMEM((chunk_count, row_count, chunk), BF16),
            pltpu.VMEM((chunk_count, row_count, chunk), F32),
            pltpu.VMEM((chunk_count, row_count, chunk), F32),
            pltpu.SemaphoreType.DMA((n_z,)),
            pltpu.SemaphoreType.DMA((n_z,)),
            pltpu.SemaphoreType.DMA,
            pltpu.SemaphoreType.DMA,
            pltpu.SemaphoreType.DMA((chunk_count,)),
            pltpu.SemaphoreType.DMA((chunk_count,)),
            pltpu.SemaphoreType.DMA((chunk_count,)),
            pltpu.SemaphoreType.DMA((chunk_count,)),
            pltpu.SemaphoreType.DMA((chunk_count,)),
        ],
        compiler_params=pltpu.CompilerParams(
            collective_id=0, has_side_effects=True, vmem_limit_bytes=48 << 20
        ),
        name="chain",
    )(heads, turned, cross, spread, cotangent)

    out_parts = jnp.stack(
        [
            jnp.einsum("ctd,th->cdh", middle, mixed_pair[0], preferred_element_type=F32),
            jnp.einsum("ctd,th->cdh", above, mixed_pair[1], preferred_element_type=F32),
        ]
    ).astype(BF16).reshape(2, half, head)
    own_back = picked(jnp.stack([backs[:, :head], backs[:, head:]]), side)
    value_parts = lax.dot_general(
        tokens, own_back, (((0,), (0,)), ((), ())), preferred_element_type=F32
    ).astype(BF16)

    grad_out, grad_value = pl.pallas_call(
        functools.partial(scatter_kernel, n_dp),
        out_shape=(jax.ShapeDtypeStruct((shard_rows, head), F32),) * 2,
        in_specs=[vmem] * 2,
        out_specs=(vmem,) * 2,
        scratch_shapes=[
            pltpu.VMEM((n_dp, shard_rows, head), BF16),
            pltpu.VMEM((n_dp, shard_rows, head), BF16),
            pltpu.SemaphoreType.DMA((2, n_dp // 2)),
            pltpu.SemaphoreType.DMA((n_dp,)),
            pltpu.SemaphoreType.DMA((n_dp,)),
            pltpu.SemaphoreType.DMA((n_dp,)),
        ],
        compiler_params=pltpu.CompilerParams(
            collective_id=1, has_side_effects=True, vmem_limit_bytes=48 << 20
        ),
        name="scatter",
    )(out_parts, value_parts)
    return (grad_input[None], grad_value[None], grad_out[None])


def solution(mesh):
    placed = (
        P("section", "dp", None),
        P("section", "dp", None, None),
        P("dp", None),
        P("dp", None),
        P("section", "dp", None),
        P("section", "dp", None),
    )
    return jax.shard_map(
        shards,
        mesh=mesh,
        in_specs=placed,
        out_specs=(P("section", "dp", None), P("section", "dp", None), P("section", "dp", None)),
        check_vma=False,
    )
```

time: 1130 us -> 547 us (0.48)
  the two profiles are of different devices: /device:TPU:32 before, /device:TPU:5 now
where the time goes in v1:
time: 547 us; the launch traced here: 546 us
  waiting for transfers between devices  363 us (66%)
  Pallas kernels  127 us (23%)
  starting transfers between devices  16.2 us (3%)
  between operations  14.1 us (3%)
  local copies, waits for them, and re-layouts  11.7 us (2%)
  matrix products  8.84 us (2%)
  other arithmetic  5.63 us (1%)
    all_gather x1, waiting for transfers between devices, shards(): value_layers = lax.all_gather(w_value[0], 'section', axis=0)  149 us
    psum x1, waiting for transfers between devices, shards(): lax.psum(jnp.einsum('tdk,dj->tkj', value_layers, w_out[0], preferred_elem...  133 us
    pallas_call x1, Pallas kernels, shards(): pl.pallas_call(functools.partial(chain_kernel, n_z, chunk_count), out_sha...  73 us
    pallas_call x1, Pallas kernels, shards(): pl.pallas_call(functools.partial(scatter_kernel, n_dp), out_shape=(jax.Sh...  54 us
    all_gather x1, waiting for transfers between devices, shards(): value_full = lax.all_gather(w_value[0], 'dp', axis=0, tiled=True)  38.5 us
    all_gather x1, waiting for transfers between devices, shards(): out_full = lax.all_gather(w_out[0], 'dp', axis=0, tiled=True)  36.2 us
    ppermute x5, starting transfers between devices, swapped(): lax.ppermute(array, 'section', [(i, i ^ 1) for i in range(n_section)])  16 us
  transfers between devices with their start and end apart: 9, of which 6 were waited for; matrix products, arithmetic and copies ran while one was open for 3% of the time, Pallas kernels for 0%

profile of v1, /device:TPU:5, one launch (start us, length us, event | category | flops | bytes accessed | tf_op | source)
XLA Modules:
  0.0 546.3 jit_solution(4296803824084053506)
XLA Ops:
  7.2 0.7 all-gather.6.cloned.1.call-update
  8.0 0.7 all-gather.10.cloned.1.call-update
  8.7 149.0 %all-gather.6.cloned.1.call-done = bf16[32,320,128]{2,1,0:T(8,128)(2,1)} async-done(((bf16[1,320,128]{2,1,0:T(8,128)(2,1)}), bf16[32,320,128]{2,1,0:T(8,128)(2,1)}) %all-gather.6.cloned.1.call-update) | async-done | bytes 2621456 | tf_op jit(solution)/shard_map/all_gather | solution.py:336
  157.7 3.8 convolution_convert_fusion.3
  161.5 0.5 all-gather.8.cloned.1.call-update
  162.4 4.6 collective-permute-start.1
  167.0 1.4 collective-permute-done.1
  168.4 38.5 %all-gather.10.cloned.1.call-done = bf16[1,5120,128]{2,1,0:T(8,128)(2,1)} async-done(((bf16[1,320,128]{2,1,0:T(8,128)(2,1)}), bf16[1,5120,128]{2,1,0:T(8,128)(2,1)}) %all-gather.10.cloned.1.call-update) | async-done | bytes 1310736 | tf_op jit(solution)/shard_map/all_gather | solution.py:334
  206.9 2.2 constant_dynamic-slice_fusion
  209.1 2.5 collective-permute-start.3
  211.6 133.1 %all-reduce.2.cloned.1.call-done = bf16[16,256,128]{2,1,0:T(8,128)(2,1)} async-done(((bf16[16,256,128]{2,1,0:T(8,128)(2,1)}), bf16[16,256,128]{2,1,0:T(8,128)(2,1)}) %all-reduce.2.cloned.1.call-update) | async-done | bytes 1048592 | tf_op jit(solution)/shard_map/psum | solution.py:337
  344.8 2.5 collective-permute-start.2
  347.3 1.8 fusion.14
  349.3 4.3 collective-permute-start.4
  353.6 36.2 %all-gather.8.cloned.1.call-done = bf16[1,5120,128]{2,1,0:T(8,128)(2,1)} async-done(((bf16[1,320,128]{2,1,0:T(8,128)(2,1)}), bf16[1,5120,128]{2,1,0:T(8,128)(2,1)}) %all-gather.8.cloned.1.call-update) | async-done | bytes 1310736 | tf_op jit(solution)/shard_map/all_gather | solution.py:335
  389.8 1.8 fusion.9
  391.6 2.1 collective-permute-start
  393.7 1.1 copy.22
  394.8 2.9 collective-permute-done
  397.8 2.2 copy.23
  400.0 1.7 fusion.4.spread_ref
  401.7 3.6 maximum_select_fusion.cross_ref
  405.3 73.0 %chain.1 = (bf16[128,5120]{1,0:T(8,128)(2,1)S(1)}, bf16[10,128,256]{2,1,0:T(8,128)(2,1)S(1)}, bf16[10,128,256]{2,1,0:T(8,128)(2,1)S(1)}, bf16[128,256]{1,0:T(8,128)(2,1)S(1)}) custom-call(f32[64,256]{1,0:T(8,128)S(1)} %maximum_select_fusion.2.heads_ref, bf16[2,64,64]{2,1,0:T(8,128)(2,1)S(1)} %maximum_select_fusion.4.probs_ref, ...), custom_call_target="tpu_custom_call" | custom-call | tf_op jit(solution)/shard_map/chain/pallas_call | solution.py:365
  478.3 1.0 copy-done.2
  479.3 0.9 copy-done.4
  480.2 1.4 copy.26
  481.6 0.3 copy.28
  482.7 0.6 fusion.1.value_ref
  483.4 54.0 %scatter.1 = (f32[320,128]{1,0:T(8,128)S(1)}, f32[320,128]{1,0:T(8,128)S(1)}) custom-call(bf16[2,2560,128]{2,1,0:T(8,128)(2,1)S(1)} %pad_maximum_fusion.out_ref, bf16[5120,128]{1,0:T(8,128)(2,1)S(1)} %fusion.1.value_ref), custom_call_target="tpu_custom_call" | custom-call | tf_op jit(solution)/shard_map/scatter/pallas_call | solution.py:408
  537.4 1.1 copy.36
  538.5 0.7 copy.37
  539.1 0.7 copy.38
  (38 shorter events, 1.5 us)
Async XLA Ops:
  7.2 340.1 %copy-start = (bf16[1,128,5120]{2,1,0:T(8,128)(2,1)S(1)}, bf16[1,128,5120]{2,1,0:T(8,128)(2,1)}, u32[]{:S(2)}) copy-start(bf16[1,128,5120]{2,1,0:T(8,128)(2,1)} %param.6) | copy-start | bytes 3932164
  7.2 150.5 %all-gather.6.cloned.1.call-start = ((), (), s32[]{:S(2)}) async-start(), calls=%async_computation | async-start | bytes 2703360 | tf_op jit(solution)/shard_map/all_gather | solution.py:336
  7.9 199.0 %all-gather.10.cloned.1.call-start = ((), (), s32[]{:S(2)}) async-start(), calls=%async_computation.3 | async-start | bytes 1392640 | tf_op jit(solution)/shard_map/all_gather | solution.py:334
  8.7 153.4 %copy-start.7 = (f32[1,2,64,64]{3,2,1,0:T(8,128)S(1)}, f32[1,2,64,64]{3,2,1,0:T(8,128)}, u32[]{:S(2)}) copy-start(f32[1,2,64,64]{3,2,1,0:T(8,128)} %param.7) | copy-start | bytes 98308
  8.7 336.1 %all-reduce.2.cloned.1.call-start = ((), (), s32[]{:S(2)}) async-start(), calls=%async_computation.1 | async-start | bytes 2097152 | tf_op jit(solution)/shard_map/psum | solution.py:337
  161.5 0.8 copy-start.8
  161.5 228.3 %all-gather.8.cloned.1.call-start = ((), (), s32[]{:S(2)}) async-start(), calls=%async_computation.2 | async-start | bytes 1392640 | tf_op jit(solution)/shard_map/all_gather | solution.py:335
  162.4 6.0 %collective-permute-start.1 = (bf16[64,64]{1,0:T(8,128)(2,1)S(1)}, bf16[64,64]{1,0:T(8,128)(2,1)S(1)}, u32[]{:S(2)}, u32[]{:S(2)}) collective-permute-start(bf16[64,64]{1,0:T(8,128)(2,1)S(1)} %get-tuple-element.22), channel_id=1, source_target_pairs={{0,16},{16,0},{32,48},{48,32},{64,80},{80,64},{96,112},{112,96},{1... | collective-permute-start | bytes 24584 | tf_op jit(solution)/shard_map/ppermute | solution.py:325
  209.1 180.7 %copy-start.1 = (bf16[128,5120]{1,0:T(8,128)(2,1)S(1)}, bf16[128,5120]{1,0:T(8,128)(2,1)}, u32[]{:S(2)}) copy-start(bf16[128,5120]{1,0:T(8,128)(2,1)} %cot_ref.1) | copy-start | bytes 3932164
  209.1 188.7 %collective-permute-start.3 = (bf16[2560,128]{1,0:T(8,128)(2,1)}, bf16[2560,128]{1,0:T(8,128)(2,1)}, u32[]{:S(2)}, u32[]{:S(2)}) collective-permute-start(bf16[2560,128]{1,0:T(8,128)(2,1)} %get-tuple-element.16), channel_id=1, source_target_pairs={{0,16},{16,0},{32,48},{48,32},{64,80},{80,64},{96,112},{112,96},{1... | collective-permute-start | bytes 1966088 | tf_op jit(solution)/shard_map/ppermute | solution.py:325
  344.8 56.9 %collective-permute-start.2 = (bf16[16,256,128]{2,1,0:T(8,128)(2,1)}, bf16[16,256,128]{2,1,0:T(8,128)(2,1)}, u32[]{:S(2)}, u32[]{:S(2)}) collective-permute-start(bf16[16,256,128]{2,1,0:T(8,128)(2,1)} %all-reduce.2.cloned.1.call-done), channel_id=1, source_target_pairs={{0,16},{16,0},{32,48},{48,32},{64,80},{80,64},{96,112},{112,96},{1... | collective-permute-start | bytes 3145736 | tf_op jit(solution)/shard_map/ppermute | solution.py:325
  349.3 45.6 %collective-permute-start.4 = (bf16[128,128]{1,0:T(8,128)(2,1)S(1)}, bf16[128,128]{1,0:T(8,128)(2,1)S(1)}, u32[]{:S(2)}, u32[]{:S(2)}) collective-permute-start(bf16[128,128]{1,0:T(8,128)(2,1)S(1)} %bitcast.93), channel_id=1, source_target_pairs={{0,16},{16,0},{32,48},{48,32},{64,80},{80,64},{96,112},{112,96},{1... | collective-permute-start | bytes 98312 | tf_op jit(solution)/shard_map/ppermute | solution.py:325
  391.6 6.2 %collective-permute-start = (f32[64,128]{1,0:T(8,128)S(1)}, f32[64,128]{1,0:T(8,128)S(1)}, u32[]{:S(2)}, u32[]{:S(2)}) collective-permute-start(f32[64,128]{1,0:T(8,128)S(1)} %get-tuple-element.20), channel_id=1, source_target_pairs={{0,16},{16,0},{32,48},{48,32},{64,80},{80,64},{96,112},{112,96},{1... | collective-permute-start | bytes 98312 | tf_op jit(solution)/shard_map/ppermute | solution.py:325
  394.8 5.1 copy-start.5
  400.0 1.7 copy-start.6
  478.3 1.1 copy-start.2
  479.3 0.9 copy-start.4
  483.4 54.0 %copy-start.3 = (bf16[128,5120]{1,0:T(8,128)(2,1)S(1)}, bf16[128,5120]{1,0:T(8,128)(2,1)}, u32[]{:S(2)}) copy-start(bf16[128,5120]{1,0:T(8,128)(2,1)} %copy-done.2) | copy-start | bytes 3932164
Sparse Core Ops, SparseCore 0:
  11.1 146.5 all-gather.5
  159.8 47.0 all-gather.9
  210.4 134.3 all-reduce.1
  347.0 42.7 all-gather.7

commit v2 on v0

v2 whole, which is shorter than its diff:
```python
import functools

import jax
import jax.numpy as jnp
from jax import lax
from jax.experimental import pallas as pl
from jax.experimental.pallas import tpu as pltpu
from jax.sharding import PartitionSpec as P

MESH = pl.DeviceIdType.MESH
F32 = jnp.float32
BF16 = jnp.bfloat16


def masked_probs(logits, doc_ids):
    seq_len = logits.shape[-1]
    places = jnp.arange(seq_len)
    allowed = (places[None, :, None] >= places[None, None, :]) & (
        doc_ids[:, :, None] == doc_ids[:, None, :]
    )
    kept = jnp.where(allowed, logits, -jnp.inf)
    row_top = jnp.max(kept, axis=-1, keepdims=True)
    expo = jnp.where(allowed, jnp.exp(kept - row_top), jnp.zeros_like(logits))
    return (expo / jnp.sum(expo, axis=-1, keepdims=True)).astype(BF16)


def dot(a, b):
    return jnp.dot(a, b, preferred_element_type=F32)


def dot_rows(a, b):
    return lax.dot_general(a, b, (((0,), (0,)), ((), ())), preferred_element_type=F32)


def dot_lanes(a, b):
    return lax.dot_general(a, b, (((1,), (1,)), ((), ())), preferred_element_type=F32)


def kernel(
    n_z,
    n_dp,
    chunk,
    acts_ref,
    cot_ref,
    turned_ref,
    value_ref,
    outw_ref,
    grad_ref,
    sum_value_ref,
    sum_out_ref,
    out_full,
    pair_rows,
    rest_rows,
    pair_out,
    layer_rows,
    part,
    parts_in,
    cross,
    heads,
    head_away,
    turned,
    line,
    backs,
    mixed,
    delta_low,
    delta_mid,
    above,
    below,
    middle,
    other,
    out_parts,
    value_parts,
    out_in,
    value_in,
    pair_out_s,
    pair_out_r,
    turned_s,
    turned_r,
    head_s,
    head_r,
    mixed_s,
    mixed_r,
    backs_s,
    backs_r,
    layer_s,
    layer_r,
    outw_s,
    outw_r,
    value_s,
    value_r,
    near_s,
    near_r,
    part_s,
    part_r,
    cross_s,
    cross_r,
    line_s,
    line_r,
    wave_s,
    wave_r,
    grad_s,
    grad_r,
    vsum_s,
    vsum_r,
    osum_s,
    osum_r,
):
    section = lax.axis_index("section")
    me = lax.axis_index("dp")
    z, side = section // 2, section % 2
    away = 1 - side
    half_dp = n_dp // 2
    my_half, my_place = me // half_dp, me % half_dp
    rows, head = value_ref.shape
    half = rows * half_dp
    chunk_count = half // chunk
    seq = heads.shape[0]
    lower = {"section": lax.rem(z + n_z - 1, n_z) * 2 + side}
    upper = {"section": lax.rem(z + 1, n_z) * 2 + side}
    partner = {"section": z * 2 + away}
    own_lanes = pl.ds(pl.multiple_of(side * head, head), head)
    away_lanes = pl.ds(pl.multiple_of(away * head, head), head)
    own_seq = pl.ds(pl.multiple_of(side * seq, seq), seq)
    away_seq = pl.ds(pl.multiple_of(away * seq, seq), seq)

    def peer(step):
        return lax.rem(me + step, n_dp)

    def shard(place):
        return pl.ds(pl.multiple_of(place * rows, 16), rows)

    def remote(src, dst, send, recv, device):
        return pltpu.make_async_remote_copy(
            src_ref=src, dst_ref=dst, send_sem=send, recv_sem=recv, device_id=device, device_id_type=MESH
        )

    barrier = pltpu.get_barrier_semaphore()
    for device in (lower, upper):
        pl.semaphore_signal(barrier, inc=1, device_id=device, device_id_type=MESH)

    def greet(step, carry):
        for target in (0, 1):
            @pl.when((target != side) | (step > 0))
            def _():
                pl.semaphore_signal(
                    barrier, inc=1, device_id={"section": z * 2 + target, "dp": peer(step)}, device_id_type=MESH
                )
        return carry

    lax.fori_loop(0, n_dp, greet, 0)
    pl.semaphore_wait(barrier, 2 * n_dp + 1)

    pair_copy = remote(outw_ref, pair_out.at[:, own_lanes], pair_out_s, pair_out_r, partner)
    pair_copy.start()

    def layer_copy(slot, src):
        return remote(src, layer_rows.at[slot], layer_s.at[slot], layer_r.at[slot], lower)

    @pl.when(z > 0)
    def _():
        layer_copy(z, value_ref).start()

    def outw_copy(step):
        return remote(outw_ref, out_full.at[shard(me)], outw_s.at[step], outw_r.at[step], {"dp": peer(step)})

    def value_copy(step, inside):
        dst = pair_rows.at[shard(my_place), own_lanes] if inside else rest_rows.at[shard(my_place)]
        return remote(value_ref, dst, value_s.at[step], value_r.at[step], {"dp": peer(step)})

    def near_copy(step):
        return remote(
            value_ref,
            pair_rows.at[shard(my_place), own_lanes],
            near_s.at[step],
            near_r.at[my_place],
            {"section": z * 2 + away, "dp": peer(step)},
        )

    def each_step(first, do):
        def body(step, carry):
            do(step)
            return carry

        lax.fori_loop(first, n_dp, body, 0)

    def start_value(step):
        @pl.when(my_half == side)
        def _():
            value_copy(step, True).start()

        @pl.when(my_half != side)
        def _():
            value_copy(step, False).start()

    each_step(1, lambda step: outw_copy(step).start())
    turned_copy = remote(turned_ref.at[away], turned.at[side], turned_s, turned_r, partner)
    turned_copy.start()
    each_step(1, start_value)

    @pl.when(my_half == away)
    def _():
        each_step(0, lambda step: near_copy(step).start())

    turned[side] = turned_ref[side]
    out_full[shard(me)] = outw_ref[...]
    pair_out[:, own_lanes] = outw_ref[...]
    layer_rows[z] = value_ref[...]

    @pl.when(my_half == side)
    def _():
        pair_rows[shard(my_place), own_lanes] = value_ref[...]

    @pl.when(my_half != side)
    def _():
        rest_rows[shard(my_place)] = value_ref[...]

    remote(outw_ref, pair_out.at[:, away_lanes], pair_out_s, pair_out_r, partner).wait_recv()

    def part_copy(slot):
        return remote(part.at[slot], parts_in.at[me], part_s.at[slot], part_r.at[me], {"dp": slot})

    def cross_copy(step, target):
        block = cross.at[me, own_lanes]
        return remote(
            block,
            block,
            cross_s.at[target * n_dp + step],
            cross_r.at[2 * me + side],
            {"section": z * 2 + target, "dp": peer(step)},
        )

    def each_cross(do):
        for target in (0, 1):
            def at(step, target=target):
                @pl.when((target != side) | (step > 0))
                def _():
                    do(cross_copy(step, target))

            each_step(0, at)

    def sum_parts():
        def add(step, total):
            source = peer(step)
            remote(part.at[0], parts_in.at[source], part_s.at[0], part_r.at[source], {"dp": source}).wait_recv()
            return total + parts_in[source].astype(F32)

        total = lax.fori_loop(1, n_dp, add, part[me].astype(F32))
        cross[me, own_lanes] = total.astype(BF16)
        each_cross(lambda copy: copy.start())

    def cross_part(slot, carry):
        @pl.when(slot > z)
        def _():
            layer_copy(slot, layer_rows.at[slot]).wait_recv()

            @pl.when(z > 0)
            def _():
                layer_copy(slot, layer_rows.at[slot]).start()

        part[slot] = dot_rows(layer_rows[slot], pair_out[...]).astype(BF16)

        @pl.when(me != slot)
        def _():
            part_copy(slot).start()

        @pl.when((slot > z) & (me == slot - 1))
        def _():
            sum_parts()

        return carry

    lax.fori_loop(z, n_z, cross_part, 0)

    @pl.when(me == n_z - 1)
    def _():
        sum_parts()

    def outw_wait(step):
        source = lax.rem(me + n_dp - step, n_dp)
        remote(outw_ref, out_full.at[shard(source)], outw_s.at[step], outw_r.at[step], {"dp": source}).wait_recv()

    each_step(1, outw_wait)
    own_heads = dot(cot_ref[...], out_full[...])
    backs_f32 = jnp.where(side == 0, own_heads[:seq], own_heads[seq:])
    heads[:, own_lanes] = backs_f32
    head_away[...] = jnp.where(side == 0, own_heads[seq:], own_heads[:seq])
    head_copy = remote(head_away, heads.at[:, own_lanes], head_s, head_r, partner)
    head_copy.start()
    remote(head_away, heads.at[:, away_lanes], head_s, head_r, partner).wait_recv()
    remote(turned_ref.at[side], turned.at[away], turned_s, turned_r, partner).wait_recv()

    def line_copy(slot):
        return remote(line.at[slot], line.at[slot], line_s.at[slot], line_r.at[slot], lower)

    def cross_wait(slot):
        for target in (0, 1):
            @pl.when((target != side) | (me != slot))
            def _():
                block = cross.at[slot, pl.ds(target * head, head)]
                remote(block, block, cross_s.at[0], cross_r.at[2 * slot + target], partner).wait_recv()

    def take(i, total):
        slot = n_z - 1 - i
        line_copy(slot).wait_recv()

        @pl.when(z > 0)
        def _():
            line_copy(slot).start()

        cross_wait(slot)
        return total + dot(line[slot], cross[slot])

    total = lax.fori_loop(0, n_z - 1 - z, take, heads[...])
    back_top = dot(turned[1, :, :seq], total[:, head:].astype(BF16)).astype(BF16)
    cross_wait(z)
    low_head = total[:, :head] + dot(back_top, cross[z, head:, :head])
    back_low = dot(turned[0, :, :seq], low_head.astype(BF16)).astype(BF16)
    line[z, :, :head] = back_low
    line[z, :, head:] = back_top

    @pl.when(z > 0)
    def _():
        line_copy(z).start()

    backs[own_seq, :head] = back_low
    backs[own_seq, head:] = back_top
    backs_copy = remote(line.at[z], backs.at[own_seq], backs_s, backs_r, partner)
    backs_copy.start()
    remote(line.at[z], backs.at[away_seq], backs_s, backs_r, partner).wait_recv()

    def value_wait(step):
        source = lax.rem(me + n_dp - step, n_dp)
        place = shard(lax.rem(source, half_dp))

        @pl.when(source // half_dp == side)
        def _():
            dst = pair_rows.at[place, own_lanes]
            remote(value_ref, dst, value_s.at[step], value_r.at[step], {"dp": source}).wait_recv()

        @pl.when(source // half_dp != side)
        def _():
            dst = rest_rows.at[place]
            remote(value_ref, dst, value_s.at[step], value_r.at[step], {"dp": source}).wait_recv()

    each_step(1, value_wait)
    for place in range(half_dp):
        dst = pair_rows.at[pl.ds(place * rows, rows), away_lanes]
        remote(value_ref, dst, near_s.at[0], near_r.at[place], partner).wait_recv()

    for k in range(chunk_count):
        weights = pair_rows[pl.ds(k * chunk, chunk), :]
        delta_low[k] = dot_lanes(backs[...], weights)
        delta_mid[k] = dot_lanes(backs[:, head:], weights[:, head:])

    def half_lanes(which):
        return pl.ds(pl.multiple_of(which * half, 128), half)

    projected = (
        dot(acts_ref[:, half_lanes(side)], pair_rows[:, own_lanes]) + dot(acts_ref[:, half_lanes(away)], rest_rows[...])
    ).astype(BF16)
    mixed[side, :seq] = dot_rows(turned_ref[0, :, :seq], projected[:seq]).astype(BF16)
    mixed[side, seq:] = dot_rows(turned_ref[1, :, :seq], projected[seq:]).astype(BF16)
    mixed_copy = remote(mixed.at[side], mixed.at[side], mixed_s, mixed_r, partner)
    mixed_copy.start()

    def vsum_copy(step):
        return remote(
            value_parts.at[shard(peer(step))], value_in.at[step], vsum_s.at[step], vsum_r.at[step], {"dp": peer(step)}
        )

    def value_gradient():
        own_back = backs[:, own_lanes]

        def piece(k, carry):
            start = pl.multiple_of(k * chunk, 128)
            value_parts[pl.ds(start, chunk)] = dot_rows(acts_ref[:, pl.ds(start, chunk)], own_back).astype(BF16)
            return carry

        lax.fori_loop(0, 2 * chunk_count, piece, 0)
        each_step(1, lambda step: vsum_copy(step).start())

    @pl.when(z < n_z - 1)
    def _():
        value_gradient()

    remote(mixed.at[side], mixed.at[away], mixed_s, mixed_r, partner).wait_recv()

    def wave_copy(k):
        return remote(below.at[k], above.at[k], wave_s.at[k], wave_r.at[k], lower)

    def columns(which, k):
        return pl.ds(pl.multiple_of(which * half + k * chunk, 128), chunk)

    def grad_copy(k):
        return remote(other.at[k], grad_ref.at[:, columns(side, k)], grad_s.at[k], grad_r.at[k], partner)

    def osum_copy(layer, i):
        return remote(
            out_parts.at[layer, pl.ds(i * rows, rows)],
            out_in.at[me],
            osum_s.at[layer * half_dp + i],
            osum_r.at[me],
            {"section": z * 2 + layer, "dp": side * half_dp + i},
        )

    def is_own(layer, i):
        return (layer == side) & (side * half_dp + i == me)

    def osum_start(layer, i):
        @pl.when(jnp.logical_not(is_own(layer, i)))
        def _():
            osum_copy(layer, i).start()

        @pl.when(is_own(layer, i))
        def _():
            out_in[me] = out_parts[layer, pl.ds(i * rows, rows)]

    sent = 0
    for k in range(chunk_count):
        @pl.when(z == n_z - 1)
        def _():
            above[k] = cot_ref[:, columns(side, k)]

        @pl.when(z < n_z - 1)
        def _():
            wave_copy(k).wait_recv()

        taken = above[k]
        low = (taken.astype(F32) + delta_low[k]).astype(BF16)
        below[k] = low

        @pl.when(z > 0)
        def _():
            wave_copy(k).start()

        mid = (taken.astype(F32) + delta_mid[k]).astype(BF16)
        grad_ref[:, columns(side, k)] = jnp.where(side == 1, mid, low)
        other[k] = jnp.where(side == 1, low, mid)
        grad_copy(k).start()
        out_parts[0, pl.ds(k * chunk, chunk)] = dot_rows(mid, mixed[0]).astype(BF16)
        out_parts[1, pl.ds(k * chunk, chunk)] = dot_rows(taken, mixed[1]).astype(BF16)
        while (sent + 1) * rows <= (k + 1) * chunk:
            for layer in (0, 1):
                osum_start(layer, sent)
            sent += 1

    @pl.when(z == n_z - 1)
    def _():
        value_gradient()

    total = value_parts[shard(me)].astype(F32)
    for step in range(1, n_dp):
        remote(
            value_parts.at[pl.ds(0, rows)], value_in.at[step], vsum_s.at[step], vsum_r.at[step], {"dp": peer(step)}
        ).wait_recv()
        total = total + value_in[step].astype(F32)
    sum_value_ref[...] = total

    source_line = z * 2 + my_half
    total = jnp.zeros((rows, head), F32)
    for source in range(n_dp):
        @pl.when((my_half != side) | (source != me))
        def _():
            remote(
                out_parts.at[0, pl.ds(0, rows)],
                out_in.at[source],
                osum_s.at[0],
                osum_r.at[source],
                {"section": source_line, "dp": source},
            ).wait_recv()

        total = total + out_in[source].astype(F32)
    sum_out_ref[...] = total

    for k in range(chunk_count):
        grad_copy(k).wait_send()
        remote(other.at[k], grad_ref.at[:, columns(away, k)], grad_s.at[k], grad_r.at[k], partner).wait_recv()

    pair_copy.wait_send()
    turned_copy.wait_send()
    head_copy.wait_send()
    backs_copy.wait_send()
    mixed_copy.wait_send()
    each_step(1, lambda step: outw_copy(step).wait_send())
    each_step(1, lambda step: vsum_copy(step).wait_send())

    def value_sent(step):
        @pl.when(my_half == side)
        def _():
            value_copy(step, True).wait_send()

        @pl.when(my_half != side)
        def _():
            value_copy(step, False).wait_send()

    each_step(1, value_sent)

    @pl.when(my_half == away)
    def _():
        each_step(0, lambda step: near_copy(step).wait_send())

    def part_sent(slot, carry):
        @pl.when(me != slot)
        def _():
            part_copy(slot).wait_send()

        return carry

    lax.fori_loop(z, n_z, part_sent, 0)

    @pl.when((me >= z) & (me < n_z))
    def _():
        each_cross(lambda copy: copy.wait_send())

    for layer in (0, 1):
        for i in range(half_dp):
            @pl.when(jnp.logical_not(is_own(layer, i)))
            def _():
                osum_copy(layer, i).wait_send()

    @pl.when(z > 0)
    def _():
        layer_copy(z, value_ref).wait_send()

        def layer_sent(slot, carry):
            layer_copy(slot, layer_rows.at[slot]).wait_send()
            return carry

        lax.fori_loop(z + 1, n_z, layer_sent, 0)

        def line_sent(slot, carry):
            line_copy(slot).wait_send()
            return carry

        lax.fori_loop(z, n_z, line_sent, 0)
        for k in range(chunk_count):
            wave_copy(k).wait_send()


def shards(acts, scores, segments, cotangent, w_value, w_out):
    n_dp = lax.axis_size("dp")
    n_z = lax.axis_size("section") // 2
    tokens = acts[0]
    row_count, feat_width = tokens.shape
    seq_len = segments.shape[1]
    shard_rows, head = w_value.shape[1:]
    half = feat_width // 2
    chunk = 256 if half % 256 == 0 else 128
    chunks = half // chunk

    probs = masked_probs(scores[0], segments)
    turned = jnp.pad(jnp.swapaxes(probs, 1, 2), ((0, 0), (0, 0), (0, 128 - seq_len)))

    vmem = pl.BlockSpec(memory_space=pltpu.VMEM)
    dma = pltpu.SemaphoreType.DMA
    one, per_z, per_dp, per_chunk = dma, dma((n_z,)), dma((n_dp,)), dma((chunks,))
    grad_input, grad_value, grad_out = pl.pallas_call(
        functools.partial(kernel, n_z, n_dp, chunk),
        out_shape=(
            jax.ShapeDtypeStruct((row_count, feat_width), BF16),
            jax.ShapeDtypeStruct((shard_rows, head), F32),
            jax.ShapeDtypeStruct((shard_rows, head), F32),
        ),
        in_specs=[vmem] * 5,
        out_specs=(vmem,) * 3,
        scratch_shapes=[
            pltpu.VMEM((feat_width, head), BF16),
            pltpu.VMEM((half, 2 * head), BF16),
            pltpu.VMEM((half, head), BF16),
            pltpu.VMEM((shard_rows, 2 * head), BF16),
            pltpu.VMEM((n_z, shard_rows, head), BF16),
            pltpu.VMEM((n_z, head, 2 * head), BF16),
            pltpu.VMEM((n_dp, head, 2 * head), BF16),
            pltpu.VMEM((n_z, 2 * head, 2 * head), BF16),
            pltpu.VMEM((seq_len, 2 * head), F32),
            pltpu.VMEM((seq_len, head), F32),
            pltpu.VMEM((2, seq_len, 128), BF16),
            pltpu.VMEM((n_z, seq_len, 2 * head), BF16),
            pltpu.VMEM((row_count, 2 * head), BF16),
            pltpu.VMEM((2, row_count, head), BF16),
            pltpu.VMEM((chunks, row_count, chunk), F32),
            pltpu.VMEM((chunks, row_count, chunk), F32),
            pltpu.VMEM((chunks, row_count, chunk), BF16),
            pltpu.VMEM((chunks, row_count, chunk), BF16),
            pltpu.VMEM((8, 128), BF16),
            pltpu.VMEM((chunks, row_count, chunk), BF16),
            pltpu.VMEM((2, half, head), BF16),
            pltpu.VMEM((feat_width, head), BF16),
            pltpu.VMEM((n_dp, shard_rows, head), BF16),
            pltpu.VMEM((n_dp, shard_rows, head), BF16),
            *([one] * 10),
            per_z,
            per_z,
            per_dp,
            per_dp,
            per_dp,
            per_dp,
            per_dp,
            dma((n_dp // 2,)),
            per_z,
            per_dp,
            dma((2 * n_dp,)),
            dma((2 * n_z,)),
            per_z,
            per_z,
            per_chunk,
            per_chunk,
            per_chunk,
            per_chunk,
            per_dp,
            per_dp,
            per_dp,
            per_dp,
        ],
        compiler_params=pltpu.CompilerParams(
            collective_id=0, has_side_effects=True, vmem_limit_bytes=52 << 20
        ),
        name="backward",
    )(tokens, cotangent, turned, w_value[0], w_out[0])
    return (grad_input[None], grad_value[None], grad_out[None])


def solution(mesh):
    placed = (
        P("section", "dp", None),
        P("section", "dp", None, None),
        P("dp", None),
        P("dp", None),
        P("section", "dp", None),
        P("section", "dp", None),
    )
    return jax.shard_map(
        shards,
        mesh=mesh,
        in_specs=placed,
        out_specs=(P("section", "dp", None), P("section", "dp", None), P("section", "dp", None)),
        check_vma=False,
    )
```

time: 1130 us -> 365 us (0.32)
  the two profiles are of different devices: /device:TPU:32 before, /device:TPU:15 now
where the time goes in v2:
time: 365 us
  Pallas kernels  358 us (98%)
  local copies, waits for them, and re-layouts  5.09 us (1%)
    pallas_call x1, Pallas kernels, shards(): pl.pallas_call(functools.partial(kernel, n_z, n_dp, chunk), out_shape=(ja...  358 us

profile of v2, /device:TPU:15, one launch (start us, length us, event | category | flops | bytes accessed | tf_op | source)
XLA Modules:
  0.0 364.9 jit_solution(17105718830553006005)
XLA Ops:
  0.6 0.9 copy.9
  1.6 1.2 fusion.7
  2.8 0.0 copy-start
  2.8 0.9 copy-done
  3.7 0.0 copy-start.1
  3.7 0.9 copy-done.1
  4.5 357.9 %backward.1 = (bf16[128,5120]{1,0:T(8,128)(2,1)S(1)}, f32[320,128]{1,0:T(8,128)S(1)}, f32[320,128]{1,0:T(8,128)S(1)}) custom-call(bf16[128,5120]{1,0:T(8,128)(2,1)} %bitcast.20, bf16[128,5120]{1,0:T(8,128)(2,1)} %cot_ref.1, bf16[2,64,128]{2,1,0:T(8,128)(2,1)S(1)} %pad.4.turned_ref, bf16[320,128]{1,0:T(8,128)(2,1)S(1)} %bitcast.18, bf16[320,128]{1,0:T(8,128)(2,1)S(1)} %bitcast.19), custom_call_target="tpu_custom_call" | custom-call | tf_op jit(solution)/shard_map/backward/pallas_call | solution.py:557
  362.5 1.1 copy.13
  363.5 0.7 copy.14
  364.2 0.7 copy.15
  (2 shorter events, 0.0 us)
Async XLA Ops:
  2.8 0.9 copy-start
  3.7 0.9 copy-start.1

commit v3 on v2

--- a/solution.py
+++ b/solution.py
@@ -66,12 +66,15 @@
     delta_mid,
     above,
     below,
-    middle,
     other,
     out_parts,
     value_parts,
     out_in,
     value_in,
+    out_pre,
+    value_pre,
+    out_core,
+    value_core,
     pair_out_s,
     pair_out_r,
     turned_s,
@@ -86,22 +89,30 @@
     layer_r,
     outw_s,
     outw_r,
+    outw_relay,
     value_s,
     value_r,
+    value_relay,
     near_s,
     near_r,
+    near_relay,
     part_s,
     part_r,
     cross_s,
     cross_r,
+    cross_relay,
     line_s,
     line_r,
     wave_s,
     wave_r,
     grad_s,
     grad_r,
+    vcore_s,
+    vcore_r,
     vsum_s,
     vsum_r,
+    ocore_s,
+    ocore_r,
     osum_s,
     osum_r,
 ):
@@ -111,6 +122,9 @@
     away = 1 - side
     half_dp = n_dp // 2
     my_half, my_place = me // half_dp, me % half_dp
+    n_chip = n_dp // 2
+    chip, core = me // 2, me % 2
+    sibling = {"dp": me + 1 - 2 * core}
     rows, head = value_ref.shape
     half = rows * half_dp
     chunk_count = half // chunk
@@ -124,7 +138,7 @@
     away_seq = pl.ds(pl.multiple_of(away * seq, seq), seq)
 
     def peer(step):
-        return lax.rem(me + step, n_dp)
+        return lax.rem(me + 2 * step, n_dp)
 
     def shard(place):
         return pl.ds(pl.multiple_of(place * rows, 16), rows)
@@ -143,7 +157,7 @@
             @pl.when((target != side) | (step > 0))
             def _():
                 pl.semaphore_signal(
-                    barrier, inc=1, device_id={"section": z * 2 + target, "dp": peer(step)}, device_id_type=MESH
+                    barrier, inc=1, device_id={"section": z * 2 + target, "dp": lax.rem(me + step, n_dp)}, device_id_type=MESH
                 )
         return carry
 
@@ -160,12 +174,32 @@
     def _():
         layer_copy(z, value_ref).start()
 
+    def each_step(first, do):
+        def body(step, carry):
+            do(step)
+            return carry
+
+        lax.fori_loop(first, n_chip, body, 0)
+
+    def beside(step):
+        return {"dp": jnp.where(step == 0, me + 1 - 2 * core, peer(step))}
+
     def outw_copy(step):
-        return remote(outw_ref, out_full.at[shard(me)], outw_s.at[step], outw_r.at[step], {"dp": peer(step)})
-
-    def value_copy(step, inside):
-        dst = pair_rows.at[shard(my_place), own_lanes] if inside else rest_rows.at[shard(my_place)]
-        return remote(value_ref, dst, value_s.at[step], value_r.at[step], {"dp": peer(step)})
+        return remote(outw_ref, out_full.at[shard(me)], outw_s.at[step], outw_r.at[me], beside(step))
+
+    def value_spot(source, do):
+        place = shard(lax.rem(source, half_dp))
+
+        @pl.when(source // half_dp == side)
+        def _():
+            do(pair_rows.at[place, own_lanes])
+
+        @pl.when(source // half_dp != side)
+        def _():
+            do(rest_rows.at[place])
+
+    def value_copy(step, spot):
+        return remote(value_ref, spot, value_s.at[step], value_r.at[me], beside(step))
 
     def near_copy(step):
         return remote(
@@ -176,26 +210,10 @@
             {"section": z * 2 + away, "dp": peer(step)},
         )
 
-    def each_step(first, do):
-        def body(step, carry):
-            do(step)
-            return carry
-
-        lax.fori_loop(first, n_dp, body, 0)
-
-    def start_value(step):
-        @pl.when(my_half == side)
-        def _():
-            value_copy(step, True).start()
-
-        @pl.when(my_half != side)
-        def _():
-            value_copy(step, False).start()
-
-    each_step(1, lambda step: outw_copy(step).start())
+    each_step(0, lambda step: outw_copy(step).start())
     turned_copy = remote(turned_ref.at[away], turned.at[side], turned_s, turned_r, partner)
     turned_copy.start()
-    each_step(1, start_value)
+    value_spot(me, lambda spot: each_step(0, lambda step: value_copy(step, spot).start()))
 
     @pl.when(my_half == away)
     def _():
@@ -219,34 +237,25 @@
     def part_copy(slot):
         return remote(part.at[slot], parts_in.at[me], part_s.at[slot], part_r.at[me], {"dp": slot})
 
+    def cross_block(slot, target):
+        return cross.at[slot, pl.ds(pl.multiple_of(target * head, head), head)]
+
     def cross_copy(step, target):
-        block = cross.at[me, own_lanes]
-        return remote(
-            block,
-            block,
-            cross_s.at[target * n_dp + step],
-            cross_r.at[2 * me + side],
-            {"section": z * 2 + target, "dp": peer(step)},
-        )
-
-    def each_cross(do):
-        for target in (0, 1):
-            def at(step, target=target):
-                @pl.when((target != side) | (step > 0))
-                def _():
-                    do(cross_copy(step, target))
-
-            each_step(0, at)
+        spare = (step == 0) & (target == side)
+        device = {"section": z * 2 + target, "dp": jnp.where(spare, me + 1 - 2 * core, peer(step))}
+        block = cross_block(me, side)
+        return remote(block, block, cross_s.at[target * n_chip + step], cross_r.at[2 * me + side], device)
 
     def sum_parts():
         def add(step, total):
-            source = peer(step)
+            source = lax.rem(me + step, n_dp)
             remote(part.at[0], parts_in.at[source], part_s.at[0], part_r.at[source], {"dp": source}).wait_recv()
             return total + parts_in[source].astype(F32)
 
         total = lax.fori_loop(1, n_dp, add, part[me].astype(F32))
         cross[me, own_lanes] = total.astype(BF16)
-        each_cross(lambda copy: copy.start())
+        for target in (0, 1):
+            each_step(0, lambda step: cross_copy(step, target).start())
 
     def cross_part(slot, carry):
         @pl.when(slot > z)
@@ -263,23 +272,28 @@
         def _():
             part_copy(slot).start()
 
-        @pl.when((slot > z) & (me == slot - 1))
-        def _():
-            sum_parts()
-
         return carry
 
     lax.fori_loop(z, n_z, cross_part, 0)
 
-    @pl.when(me == n_z - 1)
+    def outw_wait(source):
+        remote(outw_ref, out_full.at[shard(source)], outw_s.at[0], outw_r.at[source], sibling).wait_recv()
+
+    def outw_on(step):
+        rows_in = out_full.at[shard(peer(step))]
+        return remote(rows_in, rows_in, outw_relay.at[step], outw_r.at[peer(step)], sibling)
+
+    def outw_pass(step):
+        outw_wait(peer(step))
+        outw_on(step).start()
+
+    each_step(1, outw_pass)
+
+    @pl.when((me >= z) & (me < n_z))
     def _():
         sum_parts()
 
-    def outw_wait(step):
-        source = lax.rem(me + n_dp - step, n_dp)
-        remote(outw_ref, out_full.at[shard(source)], outw_s.at[step], outw_r.at[step], {"dp": source}).wait_recv()
-
-    each_step(1, outw_wait)
+    each_step(0, lambda step: outw_wait(2 * step + 1 - core))
     own_heads = dot(cot_ref[...], out_full[...])
     backs_f32 = jnp.where(side == 0, own_heads[:seq], own_heads[seq:])
     heads[:, own_lanes] = backs_f32
@@ -292,12 +306,32 @@
     def line_copy(slot):
         return remote(line.at[slot], line.at[slot], line_s.at[slot], line_r.at[slot], lower)
 
+    def cross_on(slot, target):
+        block = cross_block(slot, target)
+        return remote(block, block, cross_relay.at[slot // 2 * 2 + target], cross_r.at[2 * slot + target], sibling)
+
+    def each_cross_on(do):
+        def at(slot, carry):
+            for target in (0, 1):
+                @pl.when((slot % 2 == core) & ((slot != me) | (target != side)))
+                def _():
+                    do(slot, target)
+
+            return carry
+
+        lax.fori_loop(z, n_z, at, 0)
+
+    def cross_pass(slot, target):
+        cross_on(slot, target).wait_recv()
+        cross_on(slot, target).start()
+
+    each_cross_on(cross_pass)
+
     def cross_wait(slot):
-        for target in (0, 1):
-            @pl.when((target != side) | (me != slot))
-            def _():
-                block = cross.at[slot, pl.ds(target * head, head)]
-                remote(block, block, cross_s.at[0], cross_r.at[2 * slot + target], partner).wait_recv()
+        @pl.when(slot % 2 != core)
+        def _():
+            for target in (0, 1):
+                cross_on(slot, target).wait_recv()
 
     def take(i, total):
         slot = n_z - 1 - i
@@ -328,24 +362,34 @@
     backs_copy.start()
     remote(line.at[z], backs.at[away_seq], backs_s, backs_r, partner).wait_recv()
 
+    def value_on(step, spot):
+        return remote(spot, spot, value_relay.at[step], value_r.at[peer(step)], sibling)
+
+    def value_pass(step):
+        def do(spot):
+            value_on(step, spot).wait_recv()
+            value_on(step, spot).start()
+
+        value_spot(peer(step), do)
+
     def value_wait(step):
-        source = lax.rem(me + n_dp - step, n_dp)
-        place = shard(lax.rem(source, half_dp))
-
-        @pl.when(source // half_dp == side)
-        def _():
-            dst = pair_rows.at[place, own_lanes]
-            remote(value_ref, dst, value_s.at[step], value_r.at[step], {"dp": source}).wait_recv()
-
-        @pl.when(source // half_dp != side)
-        def _():
-            dst = rest_rows.at[place]
-            remote(value_ref, dst, value_s.at[step], value_r.at[step], {"dp": source}).wait_recv()
-
-    each_step(1, value_wait)
-    for place in range(half_dp):
-        dst = pair_rows.at[pl.ds(place * rows, rows), away_lanes]
-        remote(value_ref, dst, near_s.at[0], near_r.at[place], partner).wait_recv()
+        source = 2 * step + 1 - core
+        value_spot(
+            source, lambda spot: remote(spot, spot, value_s.at[0], value_r.at[source], sibling).wait_recv()
+        )
+
+    def near_on(i, parity):
+        place = 2 * i + parity
+        spot = pair_rows.at[shard(place), away_lanes]
+        return remote(spot, spot, near_relay.at[i], near_r.at[place], sibling)
+
+    each_step(1, value_pass)
+    for i in range(half_dp // 2):
+        near_on(i, core).wait_recv()
+        near_on(i, core).start()
+    each_step(0, value_wait)
+    for i in range(half_dp // 2):
+        near_on(i, 1 - core).wait_recv()
 
     for k in range(chunk_count):
         weights = pair_rows[pl.ds(k * chunk, chunk), :]
@@ -363,27 +407,42 @@
     mixed_copy = remote(mixed.at[side], mixed.at[side], mixed_s, mixed_r, partner)
     mixed_copy.start()
 
+    def vcore_copy(i):
+        return remote(
+            value_parts.at[shard(2 * i + 1 - core)], value_core.at[i], vcore_s.at[i], vcore_r.at[i], sibling
+        )
+
     def vsum_copy(step):
-        return remote(
-            value_parts.at[shard(peer(step))], value_in.at[step], vsum_s.at[step], vsum_r.at[step], {"dp": peer(step)}
-        )
+        to = peer(step)
+        return remote(value_pre.at[to // 2], value_in.at[chip], vsum_s.at[step], vsum_r.at[chip], {"dp": to})
 
     def value_gradient():
         own_back = backs[:, own_lanes]
-
-        def piece(k, carry):
-            start = pl.multiple_of(k * chunk, 128)
-            value_parts[pl.ds(start, chunk)] = dot_rows(acts_ref[:, pl.ds(start, chunk)], own_back).astype(BF16)
-            return carry
-
-        lax.fori_loop(0, 2 * chunk_count, piece, 0)
-        each_step(1, lambda step: vsum_copy(step).start())
+        for k in range(2 * chunk_count):
+            value_parts[pl.ds(k * chunk, chunk)] = dot_rows(acts_ref[:, pl.ds(k * chunk, chunk)], own_back).astype(BF16)
+        each_step(0, lambda i: vcore_copy(i).start())
+
+    def value_send():
+        def at(step):
+            to = peer(step)
+            vcore_copy(to // 2).wait_recv()
+            value_pre[to // 2] = (value_parts[shard(to)].astype(F32) + value_core[to // 2].astype(F32)).astype(BF16)
+
+            @pl.when(step > 0)
+            def _():
+                vsum_copy(step).start()
+
+        each_step(0, at)
 
     @pl.when(z < n_z - 1)
     def _():
         value_gradient()
 
     remote(mixed.at[side], mixed.at[away], mixed_s, mixed_r, partner).wait_recv()
+
+    @pl.when(z < n_z - 1)
+    def _():
+        value_send()
 
     def wave_copy(k):
         return remote(below.at[k], above.at[k], wave_s.at[k], wave_r.at[k], lower)
@@ -394,28 +453,45 @@
     def grad_copy(k):
         return remote(other.at[k], grad_ref.at[:, columns(side, k)], grad_s.at[k], grad_r.at[k], partner)
 
+    def ocore_copy(layer, i):
+        at = layer * (half_dp // 2) + i // 2
+        return remote(
+            out_parts.at[layer, pl.ds(i * rows, rows)], out_core.at[at], ocore_s.at[at], ocore_r.at[at], sibling
+        )
+
     def osum_copy(layer, i):
-        return remote(
-            out_parts.at[layer, pl.ds(i * rows, rows)],
-            out_in.at[me],
-            osum_s.at[layer * half_dp + i],
-            osum_r.at[me],
-            {"section": z * 2 + layer, "dp": side * half_dp + i},
-        )
+        at = layer * (half_dp // 2) + i // 2
+        device = {"section": z * 2 + layer, "dp": side * half_dp + i}
+        return remote(out_pre.at[at], out_in.at[chip], osum_s.at[at], osum_r.at[chip], device)
 
     def is_own(layer, i):
         return (layer == side) & (side * half_dp + i == me)
 
-    def osum_start(layer, i):
-        @pl.when(jnp.logical_not(is_own(layer, i)))
-        def _():
-            osum_copy(layer, i).start()
-
-        @pl.when(is_own(layer, i))
-        def _():
-            out_in[me] = out_parts[layer, pl.ds(i * rows, rows)]
-
-    sent = 0
+    def out_share(i):
+        @pl.when(i % 2 != core)
+        def _():
+            for layer in (0, 1):
+                ocore_copy(layer, i).start()
+
+    def out_send(i):
+        @pl.when(i % 2 == core)
+        def _():
+            for layer in (0, 1):
+                at = layer * (half_dp // 2) + i // 2
+                ocore_copy(layer, i).wait_recv()
+                out_pre[at] = (
+                    out_parts[layer, pl.ds(i * rows, rows)].astype(F32) + out_core[at].astype(F32)
+                ).astype(BF16)
+
+                @pl.when(jnp.logical_not(is_own(layer, i)))
+                def _():
+                    osum_copy(layer, i).start()
+
+                @pl.when(is_own(layer, i))
+                def _():
+                    out_in[chip] = out_pre[at]
+
+    shared, sent = 0, 0
     for k in range(chunk_count):
         @pl.when(z == n_z - 1)
         def _():
@@ -439,35 +515,33 @@
         grad_copy(k).start()
         out_parts[0, pl.ds(k * chunk, chunk)] = dot_rows(mid, mixed[0]).astype(BF16)
         out_parts[1, pl.ds(k * chunk, chunk)] = dot_rows(taken, mixed[1]).astype(BF16)
-        while (sent + 1) * rows <= (k + 1) * chunk:
-            for layer in (0, 1):
-                osum_start(layer, sent)
+        while sent < shared:
+            out_send(sent)
             sent += 1
+        while (shared + 1) * rows <= (k + 1) * chunk:
+            out_share(shared)
+            shared += 1
+    while sent < shared:
+        out_send(sent)
+        sent += 1
 
     @pl.when(z == n_z - 1)
     def _():
         value_gradient()
-
-    total = value_parts[shard(me)].astype(F32)
-    for step in range(1, n_dp):
-        remote(
-            value_parts.at[pl.ds(0, rows)], value_in.at[step], vsum_s.at[step], vsum_r.at[step], {"dp": peer(step)}
-        ).wait_recv()
-        total = total + value_in[step].astype(F32)
+        value_send()
+
+    total = value_pre[chip].astype(F32)
+    for step in range(1, n_chip):
+        source = peer(step) // 2
+        remote(value_pre.at[0], value_in.at[source], vsum_s.at[step], vsum_r.at[source], sibling).wait_recv()
+        total = total + value_in[source].astype(F32)
     sum_value_ref[...] = total
 
-    source_line = z * 2 + my_half
     total = jnp.zeros((rows, head), F32)
-    for source in range(n_dp):
-        @pl.when((my_half != side) | (source != me))
-        def _():
-            remote(
-                out_parts.at[0, pl.ds(0, rows)],
-                out_in.at[source],
-                osum_s.at[0],
-                osum_r.at[source],
-                {"section": source_line, "dp": source},
-            ).wait_recv()
+    for source in range(n_chip):
+        @pl.when((my_half != side) | (source != chip))
+        def _():
+            remote(out_pre.at[0], out_in.at[source], osum_s.at[0], osum_r.at[source], sibling).wait_recv()
 
         total = total + out_in[source].astype(F32)
     sum_out_ref[...] = total
@@ -481,23 +555,20 @@
     head_copy.wait_send()
     backs_copy.wait_send()
     mixed_copy.wait_send()
-    each_step(1, lambda step: outw_copy(step).wait_send())
+    each_step(0, lambda step: outw_copy(step).wait_send())
+    each_step(1, lambda step: outw_on(step).wait_send())
+    value_spot(me, lambda spot: each_step(0, lambda step: value_copy(step, spot).wait_send()))
+    each_step(1, lambda step: value_spot(peer(step), lambda spot: value_on(step, spot).wait_send()))
+
+    @pl.when(my_half == away)
+    def _():
+        each_step(0, lambda step: near_copy(step).wait_send())
+
+    for i in range(half_dp // 2):
+        near_on(i, core).wait_send()
+    each_step(0, lambda i: vcore_copy(i).wait_send())
     each_step(1, lambda step: vsum_copy(step).wait_send())
-
-    def value_sent(step):
-        @pl.when(my_half == side)
-        def _():
-            value_copy(step, True).wait_send()
-
-        @pl.when(my_half != side)
-        def _():
-            value_copy(step, False).wait_send()
-
-    each_step(1, value_sent)
-
-    @pl.when(my_half == away)
-    def _():
-        each_step(0, lambda step: near_copy(step).wait_send())
+    each_cross_on(lambda slot, target: cross_on(slot, target).wait_send())
 
     def part_sent(slot, carry):
         @pl.when(me != slot)
@@ -510,11 +581,16 @@
 
     @pl.when((me >= z) & (me < n_z))
     def _():
-        each_cross(lambda copy: copy.wait_send())
+        for target in (0, 1):
+            each_step(0, lambda step: cross_copy(step, target).wait_send())
 
     for layer in (0, 1):
         for i in range(half_dp):
-            @pl.when(jnp.logical_not(is_own(layer, i)))
+            @pl.when(i % 2 != core)
+            def _():
+                ocore_copy(layer, i).wait_send()
+
+            @pl.when((i % 2 == core) & jnp.logical_not(is_own(layer, i)))
             def _():
                 osum_copy(layer, i).wait_send()
 
@@ -553,7 +629,7 @@
 
     vmem = pl.BlockSpec(memory_space=pltpu.VMEM)
     dma = pltpu.SemaphoreType.DMA
-    one, per_z, per_dp, per_chunk = dma, dma((n_z,)), dma((n_dp,)), dma((chunks,))
+    one, per_z, per_dp, per_chunk, per_chip = dma, dma((n_z,)), dma((n_dp,)), dma((chunks,)), dma((n_dp // 2,))
     grad_input, grad_value, grad_out = pl.pallas_call(
         functools.partial(kernel, n_z, n_dp, chunk),
         out_shape=(
@@ -582,35 +658,46 @@
             pltpu.VMEM((chunks, row_count, chunk), F32),
             pltpu.VMEM((chunks, row_count, chunk), BF16),
             pltpu.VMEM((chunks, row_count, chunk), BF16),
-            pltpu.VMEM((8, 128), BF16),
             pltpu.VMEM((chunks, row_count, chunk), BF16),
             pltpu.VMEM((2, half, head), BF16),
             pltpu.VMEM((feat_width, head), BF16),
-            pltpu.VMEM((n_dp, shard_rows, head), BF16),
-            pltpu.VMEM((n_dp, shard_rows, head), BF16),
+            pltpu.VMEM((n_dp // 2, shard_rows, head), BF16),
+            pltpu.VMEM((n_dp // 2, shard_rows, head), BF16),
+            pltpu.VMEM((n_dp // 2, shard_rows, head), BF16),
+            pltpu.VMEM((n_dp // 2, shard_rows, head), BF16),
+            pltpu.VMEM((n_dp // 2, shard_rows, head), BF16),
+            pltpu.VMEM((n_dp // 2, shard_rows, head), BF16),
             *([one] * 10),
             per_z,
             per_z,
+            per_chip,
+            per_dp,
+            per_chip,
+            per_chip,
+            per_dp,
+            per_chip,
+            per_chip,
+            per_chip,
+            per_chip,
+            per_z,
             per_dp,
             per_dp,
-            per_dp,
-            per_dp,
-            per_dp,
-            dma((n_dp // 2,)),
+            dma((2 * n_z,)),
             per_z,
-            per_dp,
-            dma((2 * n_dp,)),
-            dma((2 * n_z,)),
             per_z,
             per_z,
             per_chunk,
             per_chunk,
             per_chunk,
             per_chunk,
-            per_dp,
-            per_dp,
-            per_dp,
-            per_dp,
+            per_chip,
+            per_chip,
+            per_chip,
+            per_chip,
+            per_chip,
+            per_chip,
+            per_chip,
+            per_chip,
         ],
         compiler_params=pltpu.CompilerParams(
             collective_id=0, has_side_effects=True, vmem_limit_bytes=52 << 20

time: 365 us -> 167 us (0.46)
  the two profiles are of different devices: /device:TPU:15 before, /device:TPU:27 now
where the time goes in v3:
time: 167 us
  Pallas kernels  160 us (96%)
  local copies, waits for them, and re-layouts  5.09 us (3%)
    pallas_call x1, Pallas kernels, shards(): pl.pallas_call(functools.partial(kernel, n_z, n_dp, chunk), out_shape=(ja...  160 us
    unnamed x8, local copies, waits for them, and re-layouts  5.08 us

profile of v3, /device:TPU:27, one launch (start us, length us, event | category | flops | bytes accessed | tf_op | source)
XLA Modules:
  0.0 166.5 jit_solution(13335237610012839359)
XLA Ops:
  0.6 0.9 copy.9
  1.6 1.2 fusion.7
  2.8 0.0 copy-start
  2.8 0.9 copy-done
  3.7 0.0 copy-start.1
  3.7 0.9 copy-done.1
  4.5 159.6 %backward.1 = (bf16[128,5120]{1,0:T(8,128)(2,1)S(1)}, f32[320,128]{1,0:T(8,128)S(1)}, f32[320,128]{1,0:T(8,128)S(1)}) custom-call(bf16[128,5120]{1,0:T(8,128)(2,1)} %bitcast.20, bf16[128,5120]{1,0:T(8,128)(2,1)} %cot_ref.1, bf16[2,64,128]{2,1,0:T(8,128)(2,1)S(1)} %pad.4.turned_ref, bf16[320,128]{1,0:T(8,128)(2,1)S(1)} %bitcast.18, bf16[320,128]{1,0:T(8,128)(2,1)S(1)} %bitcast.19), custom_call_target="tpu_custom_call" | custom-call | tf_op jit(solution)/shard_map/backward/pallas_call | solution.py:633
  164.1 1.1 copy.13
  165.2 0.7 copy.14
  165.9 0.7 copy.15
  (2 shorter events, 0.0 us)
Async XLA Ops:
  2.8 0.9 copy-start
  3.7 0.9 copy-start.1

commit v4 on v3

--- a/solution.py
+++ b/solution.py
@@ -58,6 +58,8 @@
     cross,
     heads,
     head_away,
+    ahead,
+    newest,
     turned,
     line,
     backs,
@@ -87,6 +89,7 @@
     backs_r,
     layer_s,
     layer_r,
+    climb_s,
     outw_s,
     outw_r,
     outw_relay,
@@ -103,6 +106,7 @@
     cross_relay,
     line_s,
     line_r,
+    next_s,
     wave_s,
     wave_r,
     grad_s,
@@ -125,12 +129,23 @@
     n_chip = n_dp // 2
     chip, core = me // 2, me % 2
     sibling = {"dp": me + 1 - 2 * core}
+
+    n_y = n_dp // 4
+
+    def summer(slot):
+        turn = n_z - 1 - slot
+        y = lax.rem(turn, n_y)
+        return 4 * y + 2 * lax.rem(y + turn // n_y, 2) + lax.rem(turn // (2 * n_y), 2)
+
+    my_slot = n_z - 1 - (me // 4 + n_y * (lax.rem(me // 2 + me // 4, 2) + 2 * core))
     rows, head = value_ref.shape
     half = rows * half_dp
     chunk_count = half // chunk
     seq = heads.shape[0]
     lower = {"section": lax.rem(z + n_z - 1, n_z) * 2 + side}
     upper = {"section": lax.rem(z + 1, n_z) * 2 + side}
+    lower_two = {"section": lax.rem(z + n_z - 2, n_z) * 2 + side}
+    upper_two = {"section": lax.rem(z + 2, n_z) * 2 + side}
     partner = {"section": z * 2 + away}
     own_lanes = pl.ds(pl.multiple_of(side * head, head), head)
     away_lanes = pl.ds(pl.multiple_of(away * head, head), head)
@@ -149,7 +164,7 @@
         )
 
     barrier = pltpu.get_barrier_semaphore()
-    for device in (lower, upper):
+    for device in (lower, upper, lower_two, upper_two):
         pl.semaphore_signal(barrier, inc=1, device_id=device, device_id_type=MESH)
 
     def greet(step, carry):
@@ -162,7 +177,14 @@
         return carry
 
     lax.fori_loop(0, n_dp, greet, 0)
-    pl.semaphore_wait(barrier, 2 * n_dp + 1)
+    reach = n_z // 2
+
+    @pl.when(z == 0)
+    def _():
+        for above_z in range(reach + 1, n_z):
+            pl.semaphore_signal(barrier, inc=1, device_id={"section": above_z * 2 + side}, device_id_type=MESH)
+
+    pl.semaphore_wait(barrier, 2 * n_dp + 3 + jnp.where(z > reach, 1, 0))
 
     pair_copy = remote(outw_ref, pair_out.at[:, own_lanes], pair_out_s, pair_out_r, partner)
     pair_copy.start()
@@ -170,9 +192,19 @@
     def layer_copy(slot, src):
         return remote(src, layer_rows.at[slot], layer_s.at[slot], layer_r.at[slot], lower)
 
+    def climb_copy(slot, src):
+        return remote(src, layer_rows.at[slot], climb_s.at[slot], layer_r.at[slot], upper)
+
+    def top_copy():
+        return remote(value_ref, layer_rows.at[z], climb_s.at[z], layer_r.at[z], {"section": side})
+
     @pl.when(z > 0)
     def _():
         layer_copy(z, value_ref).start()
+
+    @pl.when(z > reach)
+    def _():
+        top_copy().start()
 
     def each_step(first, do):
         def body(step, carry):
@@ -213,11 +245,19 @@
     each_step(0, lambda step: outw_copy(step).start())
     turned_copy = remote(turned_ref.at[away], turned.at[side], turned_s, turned_r, partner)
     turned_copy.start()
-    value_spot(me, lambda spot: each_step(0, lambda step: value_copy(step, spot).start()))
-
-    @pl.when(my_half == away)
-    def _():
-        each_step(0, lambda step: near_copy(step).start())
+
+    def value_start():
+        value_spot(me, lambda spot: each_step(0, lambda step: value_copy(step, spot).start()))
+
+        @pl.when(my_half == away)
+        def _():
+            each_step(0, lambda step: near_copy(step).start())
+
+    late = n_z - n_z // 4
+
+    @pl.when(z < late)
+    def _():
+        value_start()
 
     turned[side] = turned_ref[side]
     out_full[shard(me)] = outw_ref[...]
@@ -235,7 +275,7 @@
     remote(outw_ref, pair_out.at[:, away_lanes], pair_out_s, pair_out_r, partner).wait_recv()
 
     def part_copy(slot):
-        return remote(part.at[slot], parts_in.at[me], part_s.at[slot], part_r.at[me], {"dp": slot})
+        return remote(part.at[slot], parts_in.at[me], part_s.at[slot], part_r.at[me], {"dp": summer(slot)})
 
     def cross_block(slot, target):
         return cross.at[slot, pl.ds(pl.multiple_of(target * head, head), head)]
@@ -243,8 +283,8 @@
     def cross_copy(step, target):
         spare = (step == 0) & (target == side)
         device = {"section": z * 2 + target, "dp": jnp.where(spare, me + 1 - 2 * core, peer(step))}
-        block = cross_block(me, side)
-        return remote(block, block, cross_s.at[target * n_chip + step], cross_r.at[2 * me + side], device)
+        block = cross_block(my_slot, side)
+        return remote(block, block, cross_s.at[target * n_chip + step], cross_r.at[2 * my_slot + side], device)
 
     def sum_parts():
         def add(step, total):
@@ -252,29 +292,56 @@
             remote(part.at[0], parts_in.at[source], part_s.at[0], part_r.at[source], {"dp": source}).wait_recv()
             return total + parts_in[source].astype(F32)
 
-        total = lax.fori_loop(1, n_dp, add, part[me].astype(F32))
-        cross[me, own_lanes] = total.astype(BF16)
+        total = lax.fori_loop(1, n_dp, add, part[my_slot].astype(F32))
+        cross[my_slot, own_lanes] = total.astype(BF16)
         for target in (0, 1):
             each_step(0, lambda step: cross_copy(step, target).start())
 
-    def cross_part(slot, carry):
-        @pl.when(slot > z)
-        def _():
-            layer_copy(slot, layer_rows.at[slot]).wait_recv()
-
-            @pl.when(z > 0)
-            def _():
-                layer_copy(slot, layer_rows.at[slot]).start()
-
+    def cross_part(slot):
         part[slot] = dot_rows(layer_rows[slot], pair_out[...]).astype(BF16)
 
-        @pl.when(me != slot)
+        @pl.when(slot != my_slot)
         def _():
             part_copy(slot).start()
 
+    def goes_down(k):
+        return (z > 0) & (z + k < n_z) & (k < reach)
+
+    def climbing(k):
+        here = (k < reach) & (k > z)
+        return lax.rem(z - k + n_z, n_z), here, here & (k + 1 < reach)
+
+    def gather_step(k, carry):
+        slot, here, onward = climbing(k)
+
+        @pl.when(z + k < n_z)
+        def _():
+            layer_copy(z + k, layer_rows.at[z + k]).wait_recv()
+
+        @pl.when(goes_down(k))
+        def _():
+            layer_copy(z + k, layer_rows.at[z + k]).start()
+
+        @pl.when(here)
+        def _():
+            climb_copy(slot, layer_rows.at[slot]).wait_recv()
+
+        @pl.when(onward)
+        def _():
+            climb_copy(slot, layer_rows.at[slot]).start()
+
+        @pl.when(z + k < n_z)
+        def _():
+            cross_part(z + k)
+
+        @pl.when(here)
+        def _():
+            cross_part(slot)
+
         return carry
 
-    lax.fori_loop(z, n_z, cross_part, 0)
+    cross_part(z)
+    lax.fori_loop(1, reach + 1, gather_step, 0)
 
     def outw_wait(source):
         remote(outw_ref, out_full.at[shard(source)], outw_s.at[0], outw_r.at[source], sibling).wait_recv()
@@ -288,10 +355,6 @@
         outw_on(step).start()
 
     each_step(1, outw_pass)
-
-    @pl.when((me >= z) & (me < n_z))
-    def _():
-        sum_parts()
 
     each_step(0, lambda step: outw_wait(2 * step + 1 - core))
     own_heads = dot(cot_ref[...], out_full[...])
@@ -300,20 +363,32 @@
     head_away[...] = jnp.where(side == 0, own_heads[seq:], own_heads[:seq])
     head_copy = remote(head_away, heads.at[:, own_lanes], head_s, head_r, partner)
     head_copy.start()
+
+    @pl.when(my_slot >= z)
+    def _():
+        sum_parts()
+
+    @pl.when(z >= late)
+    def _():
+        value_start()
+
     remote(head_away, heads.at[:, away_lanes], head_s, head_r, partner).wait_recv()
     remote(turned_ref.at[side], turned.at[away], turned_s, turned_r, partner).wait_recv()
 
     def line_copy(slot):
-        return remote(line.at[slot], line.at[slot], line_s.at[slot], line_r.at[slot], lower)
+        return remote(line.at[slot], line.at[slot], line_s.at[slot], line_r.at[slot], lower_two)
+
+    def next_copy():
+        return remote(line.at[z], line.at[z], next_s, line_r.at[z], lower)
 
     def cross_on(slot, target):
         block = cross_block(slot, target)
-        return remote(block, block, cross_relay.at[slot // 2 * 2 + target], cross_r.at[2 * slot + target], sibling)
+        return remote(block, block, cross_relay.at[2 * slot + target], cross_r.at[2 * slot + target], sibling)
 
     def each_cross_on(do):
         def at(slot, carry):
             for target in (0, 1):
-                @pl.when((slot % 2 == core) & ((slot != me) | (target != side)))
+                @pl.when((summer(slot) % 2 == core) & ((slot != my_slot) | (target != side)))
                 def _():
                     do(slot, target)
 
@@ -326,41 +401,6 @@
         cross_on(slot, target).start()
 
     each_cross_on(cross_pass)
-
-    def cross_wait(slot):
-        @pl.when(slot % 2 != core)
-        def _():
-            for target in (0, 1):
-                cross_on(slot, target).wait_recv()
-
-    def take(i, total):
-        slot = n_z - 1 - i
-        line_copy(slot).wait_recv()
-
-        @pl.when(z > 0)
-        def _():
-            line_copy(slot).start()
-
-        cross_wait(slot)
-        return total + dot(line[slot], cross[slot])
-
-    total = lax.fori_loop(0, n_z - 1 - z, take, heads[...])
-    back_top = dot(turned[1, :, :seq], total[:, head:].astype(BF16)).astype(BF16)
-    cross_wait(z)
-    low_head = total[:, :head] + dot(back_top, cross[z, head:, :head])
-    back_low = dot(turned[0, :, :seq], low_head.astype(BF16)).astype(BF16)
-    line[z, :, :head] = back_low
-    line[z, :, head:] = back_top
-
-    @pl.when(z > 0)
-    def _():
-        line_copy(z).start()
-
-    backs[own_seq, :head] = back_low
-    backs[own_seq, head:] = back_top
-    backs_copy = remote(line.at[z], backs.at[own_seq], backs_s, backs_r, partner)
-    backs_copy.start()
-    remote(line.at[z], backs.at[away_seq], backs_s, backs_r, partner).wait_recv()
 
     def value_on(step, spot):
         return remote(spot, spot, value_relay.at[step], value_r.at[peer(step)], sibling)
@@ -383,29 +423,112 @@
         spot = pair_rows.at[shard(place), away_lanes]
         return remote(spot, spot, near_relay.at[i], near_r.at[place], sibling)
 
-    each_step(1, value_pass)
-    for i in range(half_dp // 2):
-        near_on(i, core).wait_recv()
-        near_on(i, core).start()
-    each_step(0, value_wait)
-    for i in range(half_dp // 2):
-        near_on(i, 1 - core).wait_recv()
-
+    def half_lanes(which):
+        return pl.ds(pl.multiple_of(which * half, 128), half)
+
+    mixed_copy = remote(mixed.at[side], mixed.at[side], mixed_s, mixed_r, partner)
+
+    def mix():
+        each_step(1, value_pass)
+        for i in range(half_dp // 2):
+            near_on(i, core).wait_recv()
+            near_on(i, core).start()
+        each_step(0, value_wait)
+        for i in range(half_dp // 2):
+            near_on(i, 1 - core).wait_recv()
+        projected = (
+            dot(acts_ref[:, half_lanes(side)], pair_rows[:, own_lanes]) + dot(acts_ref[:, half_lanes(away)], rest_rows[...])
+        ).astype(BF16)
+        mixed[side, :seq] = dot_rows(turned_ref[0, :, :seq], projected[:seq]).astype(BF16)
+        mixed[side, seq:] = dot_rows(turned_ref[1, :, :seq], projected[seq:]).astype(BF16)
+        mixed_copy.start()
+
+    early = n_z // 2 - 2
+
+    @pl.when(z < early)
+    def _():
+        mix()
+
+    def mix_late():
+        @pl.when(z >= early)
+        def _():
+            mix()
+
+    def cross_wait(slot):
+        @pl.when(summer(slot) % 2 != core)
+        def _():
+            for target in (0, 1):
+                cross_on(slot, target).wait_recv()
+
+    def line_on(slot):
+        @pl.when(z > 1)
+        def _():
+            line_copy(slot).start()
+
+    def take(i, total):
+        slot = n_z - 1 - i
+        line_copy(slot).wait_recv()
+        line_on(slot)
+        cross_wait(slot)
+        return total + dot(line[slot], cross[slot])
+
+    cross_wait(z)
+    inner = cross[z, head:, :head]
+    twice = dot(turned[0, :, :seq], turned[1, :, :seq]).astype(BF16)
+    low_turned = jnp.concatenate([turned[0, :, :seq], twice], axis=1)
+
+    @pl.when(z < n_z - 1)
+    def _():
+        cross_wait(z + 1)
+        ahead[:, : 2 * head] = cross[z + 1]
+        ahead[:, 2 * head :] = dot(cross[z + 1, :, head:], inner).astype(BF16)
+
+    total = lax.fori_loop(0, n_z - 2 - z, take, heads[...])
+    crossed = dot(total[:, head:].astype(BF16), inner)
+
+    @pl.when(z == n_z - 1)
+    def _():
+        newest[...] = jnp.zeros_like(newest)
+
+    @pl.when(z < n_z - 1)
+    def _():
+        line_copy(z + 1).wait_recv()
+        newest[...] = dot(line[z + 1], ahead[...])
+
+    low_head = (total[:, :head] + newest[:, :head]).astype(BF16)
+    top_head = (total[:, head:] + newest[:, head : 2 * head]).astype(BF16)
+    crossed = (crossed + newest[:, 2 * head :]).astype(BF16)
+    back_top = dot(turned[1, :, :seq], top_head).astype(BF16)
+    back_low = dot(low_turned, jnp.concatenate([low_head, crossed], axis=0)).astype(BF16)
+    line[z, :, :head] = back_low
+    line[z, :, head:] = back_top
+
+    @pl.when(z > 0)
+    def _():
+        next_copy().start()
+
+    backs[own_seq, :head] = back_low
+    backs[own_seq, head:] = back_top
+    backs_copy = remote(line.at[z], backs.at[own_seq], backs_s, backs_r, partner)
+    backs_copy.start()
+
+    @pl.when(z > 0)
+    def _():
+        next_copy().wait_send()
+
+    line_on(z)
+
+    @pl.when(z < n_z - 1)
+    def _():
+        line_on(z + 1)
+
+    remote(line.at[z], backs.at[away_seq], backs_s, backs_r, partner).wait_recv()
+
+    mix_late()
     for k in range(chunk_count):
         weights = pair_rows[pl.ds(k * chunk, chunk), :]
         delta_low[k] = dot_lanes(backs[...], weights)
         delta_mid[k] = dot_lanes(backs[:, head:], weights[:, head:])
-
-    def half_lanes(which):
-        return pl.ds(pl.multiple_of(which * half, 128), half)
-
-    projected = (
-        dot(acts_ref[:, half_lanes(side)], pair_rows[:, own_lanes]) + dot(acts_ref[:, half_lanes(away)], rest_rows[...])
-    ).astype(BF16)
-    mixed[side, :seq] = dot_rows(turned_ref[0, :, :seq], projected[:seq]).astype(BF16)
-    mixed[side, seq:] = dot_rows(turned_ref[1, :, :seq], projected[seq:]).astype(BF16)
-    mixed_copy = remote(mixed.at[side], mixed.at[side], mixed_s, mixed_r, partner)
-    mixed_copy.start()
 
     def vcore_copy(i):
         return remote(
@@ -439,10 +562,6 @@
         value_gradient()
 
     remote(mixed.at[side], mixed.at[away], mixed_s, mixed_r, partner).wait_recv()
-
-    @pl.when(z < n_z - 1)
-    def _():
-        value_send()
 
     def wave_copy(k):
         return remote(below.at[k], above.at[k], wave_s.at[k], wave_r.at[k], lower)
@@ -493,6 +612,12 @@
 
     shared, sent = 0, 0
     for k in range(chunk_count):
+        if k == min(3, chunk_count - 1):
+
+            @pl.when(z < n_z - 1)
+            def _():
+                value_send()
+
         @pl.when(z == n_z - 1)
         def _():
             above[k] = cot_ref[:, columns(side, k)]
@@ -571,7 +696,7 @@
     each_cross_on(lambda slot, target: cross_on(slot, target).wait_send())
 
     def part_sent(slot, carry):
-        @pl.when(me != slot)
+        @pl.when(slot != my_slot)
         def _():
             part_copy(slot).wait_send()
 
@@ -579,7 +704,7 @@
 
     lax.fori_loop(z, n_z, part_sent, 0)
 
-    @pl.when((me >= z) & (me < n_z))
+    @pl.when(my_slot >= z)
     def _():
         for target in (0, 1):
             each_step(0, lambda step: cross_copy(step, target).wait_send())
@@ -594,23 +719,38 @@
             def _():
                 osum_copy(layer, i).wait_send()
 
+    @pl.when(z > reach)
+    def _():
+        top_copy().wait_send()
+
+    def gather_sent(k, carry):
+        slot, here, onward = climbing(k)
+
+        @pl.when(goes_down(k))
+        def _():
+            layer_copy(z + k, layer_rows.at[z + k]).wait_send()
+
+        @pl.when(onward)
+        def _():
+            climb_copy(slot, layer_rows.at[slot]).wait_send()
+
+        return carry
+
+    lax.fori_loop(1, reach + 1, gather_sent, 0)
+
     @pl.when(z > 0)
     def _():
         layer_copy(z, value_ref).wait_send()
-
-        def layer_sent(slot, carry):
-            layer_copy(slot, layer_rows.at[slot]).wait_send()
-            return carry
-
-        lax.fori_loop(z + 1, n_z, layer_sent, 0)
-
+        for k in range(chunk_count):
+            wave_copy(k).wait_send()
+
+    @pl.when(z > 1)
+    def _():
         def line_sent(slot, carry):
             line_copy(slot).wait_send()
             return carry
 
         lax.fori_loop(z, n_z, line_sent, 0)
-        for k in range(chunk_count):
-            wave_copy(k).wait_send()
 
 
 def shards(acts, scores, segments, cotangent, w_value, w_out):
@@ -650,6 +790,8 @@
             pltpu.VMEM((n_z, 2 * head, 2 * head), BF16),
             pltpu.VMEM((seq_len, 2 * head), F32),
             pltpu.VMEM((seq_len, head), F32),
+            pltpu.VMEM((2 * head, 3 * head), BF16),
+            pltpu.VMEM((seq_len, 3 * head), F32),
             pltpu.VMEM((2, seq_len, 128), BF16),
             pltpu.VMEM((n_z, seq_len, 2 * head), BF16),
             pltpu.VMEM((row_count, 2 * head), BF16),
@@ -670,6 +812,7 @@
             *([one] * 10),
             per_z,
             per_z,
+            per_z,
             per_chip,
             per_dp,
             per_chip,
@@ -683,9 +826,10 @@
             per_dp,
             per_dp,
             dma((2 * n_z,)),
+            dma((2 * n_z,)),
             per_z,
             per_z,
-            per_z,
+            one,
             per_chunk,
             per_chunk,
             per_chunk,

time: 167 us -> 152 us (0.910)
  the two profiles are of different devices: /device:TPU:27 before, /device:TPU:10 now
where the time goes in v4:
time: 152 us
  Pallas kernels  145 us (95%)
  local copies, waits for them, and re-layouts  5.09 us (3%)
    pallas_call x1, Pallas kernels, shards(): pl.pallas_call(functools.partial(kernel, n_z, n_dp, chunk), out_shape=(ja...  145 us
    unnamed x8, local copies, waits for them, and re-layouts  5.08 us

profile of v4, /device:TPU:10, one launch (start us, length us, event | category | flops | bytes accessed | tf_op | source)
XLA Modules:
  0.0 151.9 jit_solution(2976919783774801181)
XLA Ops:
  0.6 0.9 copy.9
  1.6 1.2 fusion.7
  2.8 0.0 copy-start
  2.8 0.9 copy-done
  3.7 0.0 copy-start.1
  3.7 0.9 copy-done.1
  4.5 144.9 %backward.1 = (bf16[128,5120]{1,0:T(8,128)(2,1)S(1)}, f32[320,128]{1,0:T(8,128)S(1)}, f32[320,128]{1,0:T(8,128)S(1)}) custom-call(bf16[128,5120]{1,0:T(8,128)(2,1)} %bitcast.20, bf16[128,5120]{1,0:T(8,128)(2,1)} %cot_ref.1, bf16[2,64,128]{2,1,0:T(8,128)(2,1)S(1)} %pad.4.turned_ref, bf16[320,128]{1,0:T(8,128)(2,1)S(1)} %bitcast.18, bf16[320,128]{1,0:T(8,128)(2,1)S(1)} %bitcast.19), custom_call_target="tpu_custom_call" | custom-call | tf_op jit(solution)/shard_map/backward/pallas_call | solution.py:773
  149.5 1.1 copy.13
  150.5 0.7 copy.14
  151.2 0.7 copy.15
  (2 shorter events, 0.0 us)
Async XLA Ops:
  2.8 0.9 copy-start
  3.7 0.9 copy-start.1

commit v5 on v4

--- a/solution.py
+++ b/solution.py
@@ -68,6 +68,7 @@
     delta_mid,
     above,
     below,
+    middle,
     other,
     out_parts,
     value_parts,
@@ -106,7 +107,6 @@
     cross_relay,
     line_s,
     line_r,
-    next_s,
     wave_s,
     wave_r,
     grad_s,
@@ -144,8 +144,6 @@
     seq = heads.shape[0]
     lower = {"section": lax.rem(z + n_z - 1, n_z) * 2 + side}
     upper = {"section": lax.rem(z + 1, n_z) * 2 + side}
-    lower_two = {"section": lax.rem(z + n_z - 2, n_z) * 2 + side}
-    upper_two = {"section": lax.rem(z + 2, n_z) * 2 + side}
     partner = {"section": z * 2 + away}
     own_lanes = pl.ds(pl.multiple_of(side * head, head), head)
     away_lanes = pl.ds(pl.multiple_of(away * head, head), head)
@@ -164,7 +162,7 @@
         )
 
     barrier = pltpu.get_barrier_semaphore()
-    for device in (lower, upper, lower_two, upper_two):
+    for device in (lower, upper):
         pl.semaphore_signal(barrier, inc=1, device_id=device, device_id_type=MESH)
 
     def greet(step, carry):
@@ -184,27 +182,46 @@
         for above_z in range(reach + 1, n_z):
             pl.semaphore_signal(barrier, inc=1, device_id={"section": above_z * 2 + side}, device_id_type=MESH)
 
-    pl.semaphore_wait(barrier, 2 * n_dp + 3 + jnp.where(z > reach, 1, 0))
+    pl.semaphore_wait(barrier, 2 * n_dp + 1 + jnp.where(z > reach, 1, 0))
 
     pair_copy = remote(outw_ref, pair_out.at[:, own_lanes], pair_out_s, pair_out_r, partner)
     pair_copy.start()
 
-    def layer_copy(slot, src):
-        return remote(src, layer_rows.at[slot], layer_s.at[slot], layer_r.at[slot], lower)
-
-    def climb_copy(slot, src):
-        return remote(src, layer_rows.at[slot], climb_s.at[slot], layer_r.at[slot], upper)
-
-    def top_copy():
-        return remote(value_ref, layer_rows.at[z], climb_s.at[z], layer_r.at[z], {"section": side})
+    part_rows = rows // 2
+
+    def rows_of(ref, piece):
+        return ref.at[pl.ds(piece * part_rows, part_rows)]
+
+    def stream(slot, src, sems, device):
+        return [
+            remote(
+                rows_of(src, piece),
+                rows_of(layer_rows.at[slot], piece),
+                sems.at[2 * slot + piece],
+                layer_r.at[2 * slot + piece],
+                device,
+            )
+            for piece in (0, 1)
+        ]
+
+    def layer_copies(slot, src):
+        return stream(slot, src, layer_s, lower)
+
+    def climb_copies(slot, src):
+        return stream(slot, src, climb_s, upper)
+
+    def top_copies():
+        return stream(z, value_ref, climb_s, {"section": side})
 
     @pl.when(z > 0)
     def _():
-        layer_copy(z, value_ref).start()
+        for copy in layer_copies(z, value_ref):
+            copy.start()
 
     @pl.when(z > reach)
     def _():
-        top_copy().start()
+        for copy in top_copies():
+            copy.start()
 
     def each_step(first, do):
         def body(step, carry):
@@ -274,6 +291,11 @@
 
     remote(outw_ref, pair_out.at[:, away_lanes], pair_out_s, pair_out_r, partner).wait_recv()
 
+    def used(slot, target):
+        return (slot > z) | (target == 1)
+
+    sums_here = (my_slot >= z) & used(my_slot, side)
+
     def part_copy(slot):
         return remote(part.at[slot], parts_in.at[me], part_s.at[slot], part_r.at[me], {"dp": summer(slot)})
 
@@ -300,7 +322,7 @@
     def cross_part(slot):
         part[slot] = dot_rows(layer_rows[slot], pair_out[...]).astype(BF16)
 
-        @pl.when(slot != my_slot)
+        @pl.when((slot != my_slot) & used(slot, side))
         def _():
             part_copy(slot).start()
 
@@ -316,19 +338,21 @@
 
         @pl.when(z + k < n_z)
         def _():
-            layer_copy(z + k, layer_rows.at[z + k]).wait_recv()
-
-        @pl.when(goes_down(k))
-        def _():
-            layer_copy(z + k, layer_rows.at[z + k]).start()
+            for copy in layer_copies(z + k, layer_rows.at[z + k]):
+                copy.wait_recv()
+
+                @pl.when(goes_down(k))
+                def _():
+                    copy.start()
 
         @pl.when(here)
         def _():
-            climb_copy(slot, layer_rows.at[slot]).wait_recv()
-
-        @pl.when(onward)
-        def _():
-            climb_copy(slot, layer_rows.at[slot]).start()
+            for copy in climb_copies(slot, layer_rows.at[slot]):
+                copy.wait_recv()
+
+                @pl.when(onward)
+                def _():
+                    copy.start()
 
         @pl.when(z + k < n_z)
         def _():
@@ -342,6 +366,10 @@
 
     cross_part(z)
     lax.fori_loop(1, reach + 1, gather_step, 0)
+
+    @pl.when(sums_here & (z >= late))
+    def _():
+        sum_parts()
 
     def outw_wait(source):
         remote(outw_ref, out_full.at[shard(source)], outw_s.at[0], outw_r.at[source], sibling).wait_recv()
@@ -364,7 +392,7 @@
     head_copy = remote(head_away, heads.at[:, own_lanes], head_s, head_r, partner)
     head_copy.start()
 
-    @pl.when(my_slot >= z)
+    @pl.when(sums_here & (z < late))
     def _():
         sum_parts()
 
@@ -372,14 +400,9 @@
     def _():
         value_start()
 
-    remote(head_away, heads.at[:, away_lanes], head_s, head_r, partner).wait_recv()
-    remote(turned_ref.at[side], turned.at[away], turned_s, turned_r, partner).wait_recv()
 
     def line_copy(slot):
-        return remote(line.at[slot], line.at[slot], line_s.at[slot], line_r.at[slot], lower_two)
-
-    def next_copy():
-        return remote(line.at[z], line.at[z], next_s, line_r.at[z], lower)
+        return remote(line.at[slot], line.at[slot], line_s.at[slot], line_r.at[slot], lower)
 
     def cross_on(slot, target):
         block = cross_block(slot, target)
@@ -388,7 +411,7 @@
     def each_cross_on(do):
         def at(slot, carry):
             for target in (0, 1):
-                @pl.when((summer(slot) % 2 == core) & ((slot != my_slot) | (target != side)))
+                @pl.when((summer(slot) % 2 == core) & ((slot != my_slot) | (target != side)) & used(slot, target))
                 def _():
                     do(slot, target)
 
@@ -399,8 +422,6 @@
     def cross_pass(slot, target):
         cross_on(slot, target).wait_recv()
         cross_on(slot, target).start()
-
-    each_cross_on(cross_pass)
 
     def value_on(step, spot):
         return remote(spot, spot, value_relay.at[step], value_r.at[peer(step)], sibling)
@@ -428,11 +449,13 @@
 
     mixed_copy = remote(mixed.at[side], mixed.at[side], mixed_s, mixed_r, partner)
 
-    def mix():
+    def mix_relay():
         each_step(1, value_pass)
         for i in range(half_dp // 2):
             near_on(i, core).wait_recv()
             near_on(i, core).start()
+
+    def mix():
         each_step(0, value_wait)
         for i in range(half_dp // 2):
             near_on(i, 1 - core).wait_recv()
@@ -447,21 +470,28 @@
 
     @pl.when(z < early)
     def _():
+        mix_relay()
+
+    each_cross_on(cross_pass)
+
+    @pl.when(z < early)
+    def _():
         mix()
 
     def mix_late():
         @pl.when(z >= early)
         def _():
+            mix_relay()
             mix()
 
     def cross_wait(slot):
-        @pl.when(summer(slot) % 2 != core)
-        def _():
-            for target in (0, 1):
+        for target in (0, 1):
+            @pl.when((summer(slot) % 2 != core) & used(slot, target))
+            def _():
                 cross_on(slot, target).wait_recv()
 
     def line_on(slot):
-        @pl.when(z > 1)
+        @pl.when(z > 0)
         def _():
             line_copy(slot).start()
 
@@ -472,6 +502,8 @@
         cross_wait(slot)
         return total + dot(line[slot], cross[slot])
 
+    remote(head_away, heads.at[:, away_lanes], head_s, head_r, partner).wait_recv()
+    remote(turned_ref.at[side], turned.at[away], turned_s, turned_r, partner).wait_recv()
     cross_wait(z)
     inner = cross[z, head:, :head]
     twice = dot(turned[0, :, :seq], turned[1, :, :seq]).astype(BF16)
@@ -493,6 +525,7 @@
     @pl.when(z < n_z - 1)
     def _():
         line_copy(z + 1).wait_recv()
+        line_on(z + 1)
         newest[...] = dot(line[z + 1], ahead[...])
 
     low_head = (total[:, :head] + newest[:, :head]).astype(BF16)
@@ -503,24 +536,11 @@
     line[z, :, :head] = back_low
     line[z, :, head:] = back_top
 
-    @pl.when(z > 0)
-    def _():
-        next_copy().start()
-
+    line_on(z)
     backs[own_seq, :head] = back_low
     backs[own_seq, head:] = back_top
     backs_copy = remote(line.at[z], backs.at[own_seq], backs_s, backs_r, partner)
     backs_copy.start()
-
-    @pl.when(z > 0)
-    def _():
-        next_copy().wait_send()
-
-    line_on(z)
-
-    @pl.when(z < n_z - 1)
-    def _():
-        line_on(z + 1)
 
     remote(line.at[z], backs.at[away_seq], backs_s, backs_r, partner).wait_recv()
 
@@ -545,23 +565,16 @@
             value_parts[pl.ds(k * chunk, chunk)] = dot_rows(acts_ref[:, pl.ds(k * chunk, chunk)], own_back).astype(BF16)
         each_step(0, lambda i: vcore_copy(i).start())
 
-    def value_send():
-        def at(step):
-            to = peer(step)
-            vcore_copy(to // 2).wait_recv()
-            value_pre[to // 2] = (value_parts[shard(to)].astype(F32) + value_core[to // 2].astype(F32)).astype(BF16)
-
-            @pl.when(step > 0)
-            def _():
-                vsum_copy(step).start()
-
-        each_step(0, at)
+    def value_send(step):
+        to = peer(step)
+        vcore_copy(to // 2).wait_recv()
+        value_pre[to // 2] = (value_parts[shard(to)].astype(F32) + value_core[to // 2].astype(F32)).astype(BF16)
+        if step > 0:
+            vsum_copy(step).start()
 
     @pl.when(z < n_z - 1)
     def _():
         value_gradient()
-
-    remote(mixed.at[side], mixed.at[away], mixed_s, mixed_r, partner).wait_recv()
 
     def wave_copy(k):
         return remote(below.at[k], above.at[k], wave_s.at[k], wave_r.at[k], lower)
@@ -610,42 +623,53 @@
                 def _():
                     out_in[chip] = out_pre[at]
 
-    shared, sent = 0, 0
-    for k in range(chunk_count):
-        if k == min(3, chunk_count - 1):
+    shared, sent, lag, ready = 0, 0, 2, [0, 0, 0]
+    for k in range(chunk_count + lag):
+        if k < chunk_count:
+
+            @pl.when(z == n_z - 1)
+            def _():
+                above[k] = cot_ref[:, columns(side, k)]
 
             @pl.when(z < n_z - 1)
             def _():
-                value_send()
-
-        @pl.when(z == n_z - 1)
-        def _():
-            above[k] = cot_ref[:, columns(side, k)]
-
-        @pl.when(z < n_z - 1)
-        def _():
-            wave_copy(k).wait_recv()
-
-        taken = above[k]
-        low = (taken.astype(F32) + delta_low[k]).astype(BF16)
-        below[k] = low
-
-        @pl.when(z > 0)
-        def _():
-            wave_copy(k).start()
-
-        mid = (taken.astype(F32) + delta_mid[k]).astype(BF16)
-        grad_ref[:, columns(side, k)] = jnp.where(side == 1, mid, low)
-        other[k] = jnp.where(side == 1, low, mid)
-        grad_copy(k).start()
-        out_parts[0, pl.ds(k * chunk, chunk)] = dot_rows(mid, mixed[0]).astype(BF16)
-        out_parts[1, pl.ds(k * chunk, chunk)] = dot_rows(taken, mixed[1]).astype(BF16)
-        while sent < shared:
+                wave_copy(k).wait_recv()
+
+            taken = above[k].astype(F32)
+            low = (taken + delta_low[k]).astype(BF16)
+            below[k] = low
+
+            @pl.when(z > 0)
+            def _():
+                wave_copy(k).start()
+
+            mid = (taken + delta_mid[k]).astype(BF16)
+            middle[k] = mid
+            grad_ref[:, columns(side, k)] = jnp.where(side == 1, mid, low)
+            other[k] = jnp.where(side == 1, low, mid)
+            grad_copy(k).start()
+
+        if k < lag:
+            continue
+        if k == lag:
+            remote(mixed.at[side], mixed.at[away], mixed_s, mixed_r, partner).wait_recv()
+
+        done = k - lag
+        if done < n_chip:
+
+            @pl.when(z < n_z - 1)
+            def _():
+                value_send((done + 1) % n_chip)
+
+        out_parts[0, pl.ds(done * chunk, chunk)] = dot_rows(middle[done], mixed[0]).astype(BF16)
+        out_parts[1, pl.ds(done * chunk, chunk)] = dot_rows(above[done], mixed[1]).astype(BF16)
+        while sent < ready[0]:
             out_send(sent)
             sent += 1
-        while (shared + 1) * rows <= (k + 1) * chunk:
+        while (shared + 1) * rows <= (done + 1) * chunk:
             out_share(shared)
             shared += 1
+        ready = ready[1:] + [shared]
     while sent < shared:
         out_send(sent)
         sent += 1
@@ -653,7 +677,8 @@
     @pl.when(z == n_z - 1)
     def _():
         value_gradient()
-        value_send()
+        for step in range(n_chip):
+            value_send(step)
 
     total = value_pre[chip].astype(F32)
     for step in range(1, n_chip):
@@ -696,7 +721,7 @@
     each_cross_on(lambda slot, target: cross_on(slot, target).wait_send())
 
     def part_sent(slot, carry):
-        @pl.when(slot != my_slot)
+        @pl.when((slot != my_slot) & used(slot, side))
         def _():
             part_copy(slot).wait_send()
 
@@ -704,7 +729,7 @@
 
     lax.fori_loop(z, n_z, part_sent, 0)
 
-    @pl.when(my_slot >= z)
+    @pl.when(sums_here)
     def _():
         for target in (0, 1):
             each_step(0, lambda step: cross_copy(step, target).wait_send())
@@ -721,18 +746,21 @@
 
     @pl.when(z > reach)
     def _():
-        top_copy().wait_send()
+        for copy in top_copies():
+            copy.wait_send()
 
     def gather_sent(k, carry):
         slot, here, onward = climbing(k)
 
         @pl.when(goes_down(k))
         def _():
-            layer_copy(z + k, layer_rows.at[z + k]).wait_send()
+            for copy in layer_copies(z + k, layer_rows.at[z + k]):
+                copy.wait_send()
 
         @pl.when(onward)
         def _():
-            climb_copy(slot, layer_rows.at[slot]).wait_send()
+            for copy in climb_copies(slot, layer_rows.at[slot]):
+                copy.wait_send()
 
         return carry
 
@@ -740,11 +768,12 @@
 
     @pl.when(z > 0)
     def _():
-        layer_copy(z, value_ref).wait_send()
+        for copy in layer_copies(z, value_ref):
+            copy.wait_send()
         for k in range(chunk_count):
             wave_copy(k).wait_send()
 
-    @pl.when(z > 1)
+    @pl.when(z > 0)
     def _():
         def line_sent(slot, carry):
             line_copy(slot).wait_send()
@@ -801,6 +830,7 @@
             pltpu.VMEM((chunks, row_count, chunk), BF16),
             pltpu.VMEM((chunks, row_count, chunk), BF16),
             pltpu.VMEM((chunks, row_count, chunk), BF16),
+            pltpu.VMEM((chunks, row_count, chunk), BF16),
             pltpu.VMEM((2, half, head), BF16),
             pltpu.VMEM((feat_width, head), BF16),
             pltpu.VMEM((n_dp // 2, shard_rows, head), BF16),
@@ -810,9 +840,9 @@
             pltpu.VMEM((n_dp // 2, shard_rows, head), BF16),
             pltpu.VMEM((n_dp // 2, shard_rows, head), BF16),
             *([one] * 10),
-            per_z,
-            per_z,
-            per_z,
+            dma((2 * n_z,)),
+            dma((2 * n_z,)),
+            dma((2 * n_z,)),
             per_chip,
             per_dp,
             per_chip,
@@ -829,7 +859,6 @@
             dma((2 * n_z,)),
             per_z,
             per_z,
-            one,
             per_chunk,
             per_chunk,
             per_chunk,

time: 152 us -> 151 us (level)
  no operation moved by 1% of the time
where the time goes in v5:
time: 151 us
  Pallas kernels  144 us (95%)
  local copies, waits for them, and re-layouts  5.09 us (3%)
    pallas_call x1, Pallas kernels, shards(): pl.pallas_call(functools.partial(kernel, n_z, n_dp, chunk), out_shape=(ja...  144 us
    unnamed x8, local copies, waits for them, and re-layouts  5.08 us

profile of v5, /device:TPU:10, one launch (start us, length us, event | category | flops | bytes accessed | tf_op | source)
XLA Modules:
  0.0 150.7 jit_solution(4363053861715485460)
XLA Ops:
  0.6 0.9 copy.9
  1.6 1.2 fusion.7
  2.8 0.0 copy-start
  2.8 0.9 copy-done
  3.7 0.0 copy-start.1
  3.7 0.9 copy-done.1
  4.5 143.7 %backward.1 = (bf16[128,5120]{1,0:T(8,128)(2,1)S(1)}, f32[320,128]{1,0:T(8,128)S(1)}, f32[320,128]{1,0:T(8,128)S(1)}) custom-call(bf16[128,5120]{1,0:T(8,128)(2,1)} %bitcast.20, bf16[128,5120]{1,0:T(8,128)(2,1)} %cot_ref.1, bf16[2,64,128]{2,1,0:T(8,128)(2,1)S(1)} %pad.4.turned_ref, bf16[320,128]{1,0:T(8,128)(2,1)S(1)} %bitcast.18, bf16[320,128]{1,0:T(8,128)(2,1)S(1)} %bitcast.19), custom_call_target="tpu_custom_call" | custom-call | tf_op jit(solution)/shard_map/backward/pallas_call | solution.py:802
  148.3 1.1 copy.13
  149.4 0.7 copy.14
  150.0 0.7 copy.15
  (2 shorter events, 0.0 us)
Async XLA Ops:
  2.8 0.9 copy-start
  3.7 0.9 copy-start.1

commit v6 on v5

--- a/solution.py
+++ b/solution.py
@@ -12,16 +12,15 @@
 BF16 = jnp.bfloat16
 
 
-def masked_probs(logits, doc_ids):
-    seq_len = logits.shape[-1]
-    places = jnp.arange(seq_len)
-    allowed = (places[None, :, None] >= places[None, None, :]) & (
-        doc_ids[:, :, None] == doc_ids[:, None, :]
-    )
-    kept = jnp.where(allowed, logits, -jnp.inf)
+def turned_probs(scores, ids_across, ids_down):
+    seq_len = scores.shape[0]
+    query = lax.broadcasted_iota(jnp.int32, (seq_len, seq_len), 0)
+    key = lax.broadcasted_iota(jnp.int32, (seq_len, seq_len), 1)
+    allowed = (query >= key) & (ids_down == ids_across)
+    kept = jnp.where(allowed, scores, -jnp.inf)
     row_top = jnp.max(kept, axis=-1, keepdims=True)
-    expo = jnp.where(allowed, jnp.exp(kept - row_top), jnp.zeros_like(logits))
-    return (expo / jnp.sum(expo, axis=-1, keepdims=True)).astype(BF16)
+    expo = jnp.where(allowed, jnp.exp(kept - row_top), 0.0)
+    return (expo / jnp.sum(expo, axis=-1, keepdims=True)).T.astype(BF16)
 
 
 def dot(a, b):
@@ -42,12 +41,15 @@
     chunk,
     acts_ref,
     cot_ref,
-    turned_ref,
+    scores_ref,
+    across_ref,
+    down_ref,
     value_ref,
     outw_ref,
     grad_ref,
     sum_value_ref,
     sum_out_ref,
+    turned_ref,
     out_full,
     pair_rows,
     rest_rows,
@@ -175,6 +177,9 @@
         return carry
 
     lax.fori_loop(0, n_dp, greet, 0)
+    for which in (0, 1):
+        turned_ref[which, :, :seq] = turned_probs(scores_ref[which], across_ref[which], down_ref[which])
+        turned_ref[which, :, seq:] = jnp.zeros((seq, turned_ref.shape[2] - seq), BF16)
     reach = n_z // 2
 
     @pl.when(z == 0)
@@ -793,9 +798,6 @@
     chunk = 256 if half % 256 == 0 else 128
     chunks = half // chunk
 
-    probs = masked_probs(scores[0], segments)
-    turned = jnp.pad(jnp.swapaxes(probs, 1, 2), ((0, 0), (0, 0), (0, 128 - seq_len)))
-
     vmem = pl.BlockSpec(memory_space=pltpu.VMEM)
     dma = pltpu.SemaphoreType.DMA
     one, per_z, per_dp, per_chunk, per_chip = dma, dma((n_z,)), dma((n_dp,)), dma((chunks,)), dma((n_dp // 2,))
@@ -806,9 +808,10 @@
             jax.ShapeDtypeStruct((shard_rows, head), F32),
             jax.ShapeDtypeStruct((shard_rows, head), F32),
         ),
-        in_specs=[vmem] * 5,
+        in_specs=[vmem] * 7,
         out_specs=(vmem,) * 3,
         scratch_shapes=[
+            pltpu.VMEM((2, seq_len, 128), BF16),
             pltpu.VMEM((feat_width, head), BF16),
             pltpu.VMEM((half, 2 * head), BF16),
             pltpu.VMEM((half, head), BF16),
@@ -876,7 +879,7 @@
             collective_id=0, has_side_effects=True, vmem_limit_bytes=52 << 20
         ),
         name="backward",
-    )(tokens, cotangent, turned, w_value[0], w_out[0])
+    )(tokens, cotangent, scores[0], segments[:, None, :], segments[:, :, None], w_value[0], w_out[0])
     return (grad_input[None], grad_value[None], grad_out[None])
 
 

time: 151 us -> 151 us (level)
    unnamed x8 -> x11, local copies, waits for them, and re-layouts: 5.08 us -> 5.68 us
where the time goes in v6:
time: 151 us
  Pallas kernels  144 us (95%)
  local copies, waits for them, and re-layouts  6.46 us (4%)
    pallas_call x1, Pallas kernels, shards(): pl.pallas_call(functools.partial(kernel, n_z, n_dp, chunk), out_shape=(ja...  144 us
    unnamed x11, local copies, waits for them, and re-layouts  5.68 us

profile of v6, /device:TPU:10, one launch (start us, length us, event | category | flops | bytes accessed | tf_op | source)
XLA Modules:
  0.0 151.0 jit_solution(13976157520734226392)
XLA Ops:
  0.6 0.8 copy.10.down_ref
  1.4 0.0 copy-start
  1.4 0.9 copy-done
  2.3 0.0 copy-start.1
  2.3 0.9 copy-done.1
  3.2 0.0 copy-start.2
  3.2 0.8 copy-done.2
  4.0 0.0 copy-start.3
  4.0 0.7 copy-done.3
  4.7 143.9 %backward.1 = (bf16[128,5120]{1,0:T(8,128)(2,1)S(1)}, f32[320,128]{1,0:T(8,128)S(1)}, f32[320,128]{1,0:T(8,128)S(1)}) custom-call(bf16[128,5120]{1,0:T(8,128)(2,1)} %bitcast.19, bf16[128,5120]{1,0:T(8,128)(2,1)} %cot_ref.1, f32[2,64,64]{2,1,0:T(8,128)S(1)} %bitcast.16, s32[2,1,64]{2,1,0:T(1,128)S(1)} %bitcast.18, s32[2,64,1]{2,1,0:T(8,128)S(1)} %copy.10.down_ref, ...), custom_call_target="tpu_custom_call" | custom-call | tf_op jit(solution)/shard_map/backward/pallas_call | solution.py:804
  148.7 1.1 copy.14
  149.7 0.7 copy.15
  150.4 0.7 copy.16
Async XLA Ops:
  1.4 0.9 copy-start
  2.3 0.9 copy-start.1
  3.2 0.8 copy-start.2
  4.0 0.7 copy-start.3
